TPU v7x, 256 devices: a whole 4x4x8 slice. The times are simulated.
256 devices in a mesh: prompt: 32 (over x_lo, z, core), tensor: 8 (over x_hi, y).
Axes of the slice: x: 4 (x_hi: 2, x_lo: 2; x = x_hi * 2 + x_lo), y: 4, z: 8, core: 2. Of those that a mesh axis runs over, the one named last changes fastest.
Arguments:
- state_hidden: bfloat16 [64, 128, 4096], P('prompt', None, 'tensor'), may hold values from -12 to 12
- prefix_hidden: bfloat16 [32, 1024, 4096], P('prompt', None, 'tensor'), may hold values from -12 to 12
- norm_gain: bfloat16 [4096], replicated, may hold values from 0.099609375 to 1.8984375
- w_query: bfloat16 [4096, 4096], P(None, 'tensor'), may hold values from -1 to 1
- w_key: bfloat16 [4096, 1024], P(None, 'tensor'), may hold values from -1 to 1
- w_value: bfloat16 [4096, 1024], P(None, 'tensor'), may hold values from -0.09375 to 0.09375
- w_out: bfloat16 [4096, 4096], P('tensor'), may hold values from -0.09375 to 0.09375
- scored_prompt: int32 [32, 2], P('prompt'), may hold values from 0 to 31, as said below
- prefix_len: int32 [32], replicated, may hold values from 1 to 1024, as said below
- state_mask: int32 [64, 128], P('prompt'), may hold values 0 or 1
Outputs:
- mixed: bfloat16 [64, 128, 4096], P('prompt', None, 'tensor')
Inputs may be any that keep to these rules, and one draw needn't show every extreme that they name: `scored_prompt`: each column is a permutation of the prompts, so every prompt has exactly 2 states, one in each slot. `prefix_len`: some prompt uses all 1024 positions.
All inputs are finite; a program needn't handle non-finite values. No bound on the sum of `state_mask` on one device may be relied on, other than what follows from the above.
Results may differ from a plain program's by a relative error of at most 0.017.
Values may be sent and summed in bfloat16 or wider, within the bound.
No kernel may reach another device: no remote copies, remote signals or barrier semaphores. Data moves between devices by JAX's collectives and lax.ppermute only.
A program may use at most 128 MiB of HBM per device.

v0:
```python
import jax
import jax.numpy as jnp
from jax import lax
from jax.sharding import PartitionSpec as P

HEAD_DIM = 128


def normalize(hidden, gain):
    values = hidden.astype(jnp.float32)
    scale = lax.rsqrt(jnp.mean(values * values, axis=-1, keepdims=True) + 1e-05)
    return (values * scale * gain.astype(jnp.float32)).astype(jnp.bfloat16)


def per_device(
    state_hidden,
    prefix_hidden,
    norm_gain,
    w_query,
    w_key,
    w_value,
    w_out,
    scored_prompt,
    prefix_len,
    state_mask,
):
    full_state, full_prefix = (
        lax.all_gather(state_hidden, "tensor", axis=2, tiled=True),
        lax.all_gather(prefix_hidden, "tensor", axis=2, tiled=True),
    )
    states, length, width = full_state.shape
    prefix_rows = full_prefix.shape[1]
    kv_local = w_key.shape[1] // HEAD_DIM
    heads_local = w_query.shape[1] // HEAD_DIM
    group = heads_local // kv_local
    split = kv_local * HEAD_DIM
    columns = 2 * split
    normed_state = normalize(full_state, norm_gain).reshape(-1, width)
    normed_prefix = normalize(full_prefix, norm_gain).reshape(-1, width)
    prefix_keys = jnp.dot(normed_prefix, w_key, preferred_element_type=jnp.float32).astype(
        jnp.bfloat16
    )
    prefix_values = jnp.dot(normed_prefix, w_value, preferred_element_type=jnp.float32).astype(
        jnp.bfloat16
    )
    prefix_block = jnp.concatenate([prefix_keys, prefix_values], axis=1).reshape(
        1, prefix_rows, columns
    )
    queries = (
        jnp.dot(normed_state, w_query, preferred_element_type=jnp.float32) * HEAD_DIM ** (-0.5)
    ).astype(jnp.bfloat16)
    queries = queries.reshape(states, length, kv_local, group, HEAD_DIM)
    state_keys = (
        jnp.dot(normed_state, w_key, preferred_element_type=jnp.float32)
        .astype(jnp.bfloat16)
        .reshape(states, length, kv_local, HEAD_DIM)
    )
    state_values = (
        jnp.dot(normed_state, w_value, preferred_element_type=jnp.float32)
        .astype(jnp.bfloat16)
        .reshape(states, length, kv_local, HEAD_DIM)
    )
    owners = scored_prompt[0]
    prompt_ids = jnp.arange(prefix_len.shape[0], dtype=jnp.int32)
    limits = jnp.sum(
        jnp.where(owners[:, None] == prompt_ids[None, :], prefix_len[None, :], 0), axis=1
    )
    tokens = jnp.arange(length, dtype=jnp.int32)
    causal = (tokens[None, None, :] <= tokens[None, :, None]) & (state_mask[:, None, :] == 1)
    every_block = lax.all_gather(prefix_block, "prompt", axis=0, tiled=True)
    picked = jnp.take(every_block, owners, axis=0)
    keys = jnp.concatenate(
        [picked[..., :split].reshape(states, prefix_rows, kv_local, HEAD_DIM), state_keys], axis=1
    )
    values = jnp.concatenate(
        [picked[..., split:].reshape(states, prefix_rows, kv_local, HEAD_DIM), state_values], axis=1
    )
    scores = jnp.einsum("stkgd,sjkd->skgtj", queries, keys, preferred_element_type=jnp.float32)
    valid_prefix = jnp.broadcast_to(
        (jnp.arange(prefix_rows, dtype=jnp.int32)[None, :] < limits[:, None])[:, None, :],
        (states, length, prefix_rows),
    )
    valid = jnp.concatenate([valid_prefix, causal], axis=2)[:, None, None]
    scores = jnp.where(valid, scores, -1e30)
    top = jnp.max(scores, axis=-1, keepdims=True)
    weights = jnp.where(valid, jnp.exp(scores - top), 0.0)
    numer = jnp.einsum(
        "skgtj,sjkd->stkgd",
        weights.astype(jnp.bfloat16),
        values,
        preferred_element_type=jnp.float32,
    )
    denom = jnp.transpose(jnp.sum(weights, axis=-1), (0, 3, 1, 2))[..., None]
    attended = (numer / denom).astype(jnp.bfloat16)
    flat = attended.reshape(states * length, heads_local * HEAD_DIM)
    terms = jnp.dot(flat, w_out, preferred_element_type=jnp.float32).reshape(
        states, length, w_out.shape[1]
    )
    return lax.psum_scatter(terms.astype(jnp.bfloat16), "tensor", scatter_dimension=2, tiled=True)


def solution(mesh):
    placed = (
        P("prompt", None, "tensor"),
        P("prompt", None, "tensor"),
        P(),
        P(None, "tensor"),
        P(None, "tensor"),
        P(None, "tensor"),
        P("tensor", None),
        P("prompt", None),
        P(),
        P("prompt", None),
    )
    return jax.shard_map(
        per_device,
        mesh=mesh,
        in_specs=placed,
        out_specs=P("prompt", None, "tensor"),
        check_vma=False,
    )
```

profile of v0, /device:TPU:32, one launch (start us, length us, event | category | flops | bytes accessed | tf_op | source)
XLA Modules:
  0.0 413.2 jit_solution(2702033671879474873)
XLA Ops:
  6.5 0.7 all-gather.5.cloned.1.call-update
  7.3 0.7 all-gather.7.cloned.1.call-update
  8.1 0.7 convert_element_type.41
  8.8 122.0 %all-gather.5.cloned.1.call-done = bf16[1,1024,4096]{2,1,0:T(8,128)(2,1)} async-done(((bf16[1,1024,512]{2,1,0:T(8,128)(2,1)}), bf16[1,1024,4096]{2,1,0:T(8,128)(2,1)}) %all-gather.5.cloned.1.call-update) | async-done | bytes 8388624 | tf_op jit(solution)/shard_map/all_gather | solution.py:29
  130.8 5.2 %fusion = f32[1024]{0:T(1024)S(1)} fusion(bf16[1,1024,4096]{2,1,0:T(8,128)(2,1)} %all-gather.5.cloned.1.call-done), kind=kLoop, calls=%fused_computation.3 | loop fusion | flops 12581888 | bytes 8392704 | tf_op jit(solution)/shard_map/reduce_sum | solution.py:11
  136.6 3.5 fusion.23
  140.1 3.5 fusion.26
  143.6 0.8 pad_maximum_fusion
  145.5 45.2 %all-gather.7.cloned.1.call-done = bf16[2,128,4096]{2,1,0:T(8,128)(2,1)} async-done(((bf16[2,128,512]{2,1,0:T(8,128)(2,1)}), bf16[2,128,4096]{2,1,0:T(8,128)(2,1)}) %all-gather.7.cloned.1.call-update) | async-done | bytes 2097168 | tf_op jit(solution)/shard_map/all_gather | solution.py:28
  190.7 2.2 fusion.5
  193.0 2.2 fusion.7
  195.2 2.0 fusion.22
  197.2 1.7 reshape.157
  198.9 0.7 convolution_convert_fusion.1
  199.6 2.6 convolution_convert_fusion.2
  202.2 88.2 %all-gather.9.cloned.1.call-done = bf16[32768,256]{0,1:T(8,128)(2,1)} async-done(((bf16[1024,256]{0,1:T(8,128)(2,1)}), bf16[32768,256]{0,1:T(8,128)(2,1)}) %all-gather.9.cloned.1.call-update) | async-done | bytes 16777232 | tf_op jit(solution)/shard_map/all_gather | solution.py:70
  290.3 22.3 %copy.29 = bf16[32768,256]{1,0:T(8,128)(2,1)} copy(bf16[32768,256]{0,1:T(8,128)(2,1)} %all-gather.9.cloned.1.call-done) | data formatting | bytes 33554432 | tf_op jit(solution)/shard_map/all_gather | solution.py:70
  312.7 6.4 %gather_fusion = bf16[2,1024,256]{2,1,0:T(8,128)(2,1)S(1)} fusion(bf16[32,1024,256]{2,1,0:T(8,128)(2,1)} %bitcast.93, s32[1024]{0:T(1024)S(1)} %pad_clamp_fusion), kind=kCustom, calls=%fused_computation | custom fusion | bytes 2097160 | tf_op jit(solution)/shard_map/jit(_take)/gather | solution.py:71
  319.5 0.8 fusion.4
  320.3 1.0 fusion.9
  321.3 1.0 fusion.32
  322.4 1.1 copy-done.3
  323.5 2.6 convolution_convert_fusion
  326.1 80.5 %reduce-scatter.2.cloned.1.call-done = bf16[2,128,512]{2,1,0:T(8,128)(2,1)} async-done(((bf16[2,128,4096]{2,1,0:T(8,128)(2,1)}), bf16[2,128,512]{2,1,0:T(8,128)(2,1)}) %reduce-scatter.2.cloned.1.call-update) | async-done | bytes 262160 | tf_op jit(solution)/shard_map/reduce_scatter | solution.py:99
  (41 shorter events, 2.0 us)
Async XLA Ops:
  6.5 129.5 %copy-start = (bf16[4096,128]{1,0:T(8,128)(2,1)S(1)}, bf16[4096,128]{1,0:T(8,128)(2,1)}, u32[]{:S(2)}) copy-start(bf16[4096,128]{1,0:T(8,128)(2,1)} %param.14) | copy-start | bytes 3145732
  6.5 124.3 %all-gather.5.cloned.1.call-start = ((), (), s32[]{:S(2)}) async-start(), calls=%async_computation.1 | async-start | bytes 9437184 | tf_op jit(solution)/shard_map/all_gather | solution.py:29
  7.3 183.5 %all-gather.7.cloned.1.call-start = ((), (), s32[]{:S(2)}) async-start(), calls=%async_computation.2 | async-start | bytes 2359296 | tf_op jit(solution)/shard_map/all_gather | solution.py:28
  8.0 282.3 %all-gather.9.cloned.1.call-start = ((), (), s32[]{:S(2)}) async-start(), calls=%async_computation.4 | async-start | bytes 17301504 | tf_op jit(solution)/shard_map/all_gather | solution.py:70
  130.8 5.8 %copy-start.2 = (bf16[1,1024,4096]{2,1,0:T(8,128)(2,1)S(1)}, bf16[1,1024,4096]{2,1,0:T(8,128)(2,1)}, u32[]{:S(2)}) copy-start(bf16[1,1024,4096]{2,1,0:T(8,128)(2,1)} %all-gather.5.cloned.1.call-done) | copy-start | bytes 25165828
  136.6 3.5 copy-start.4
  140.1 4.6 %copy-start.10 = (s32[1,2]{1,0:T(1,128)S(1)}, s32[1,2]{1,0:T(1,128)}, u32[]{:S(2)}) copy-start(s32[1,2]{1,0:T(1,128)} %param.17) | copy-start | bytes 28
  140.1 4.7 %copy-start.9 = (s32[32]{0:T(128)S(1)}, s32[32]{0:T(128)}, u32[]{:S(2)}) copy-start(s32[32]{0:T(128)} %param.18) | copy-start | bytes 388
  140.1 4.9 %copy-start.8 = (s32[2,128]{1,0:T(2,128)S(1)}, s32[2,128]{1,0:T(2,128)}, u32[]{:S(2)}) copy-start(s32[2,128]{1,0:T(2,128)} %param.19) | copy-start | bytes 3076
  144.5 262.2 %reduce-scatter.2.cloned.1.call-start = ((), (), s32[]{:S(2)}) async-start(), calls=%async_computation.3 | async-start | bytes 2359296 | tf_op jit(solution)/shard_map/reduce_scatter | solution.py:99
  190.7 4.5 %copy-start.7 = (bf16[4096,512]{1,0:T(8,128)(2,1)S(1)}, bf16[4096,512]{1,0:T(8,128)(2,1)}, u32[]{:S(2)}) copy-start(bf16[4096,512]{1,0:T(8,128)(2,1)} %param.13) | copy-start | bytes 12582916
  312.7 6.8 %copy-start.5 = (bf16[2,128,4,128]{3,2,1,0:T(4,128)(2,1)S(1)}, bf16[2,128,4,128]{3,2,1,0:T(4,128)(2,1)}, u32[]{:S(2)}) copy-start(bf16[2,128,4,128]{3,2,1,0:T(4,128)(2,1)} %reshape.157) | copy-start | bytes 786436
  319.5 1.8 copy-start.6
  321.3 2.2 copy-start.3
  321.3 85.3 %copy-start.1 = (bf16[4096,128]{1,0:T(8,128)(2,1)S(1)}, bf16[4096,128]{1,0:T(8,128)(2,1)}, u32[]{:S(2)}) copy-start(bf16[4096,128]{1,0:T(8,128)(2,1)} %param.14) | copy-start | bytes 3145732
Sparse Core Ops, SparseCore 0:
  9.8 120.9 all-gather.4
  133.3 57.4 all-gather.6
  192.6 97.7 all-gather.8
  326.2 80.3 reduce-scatter.1
where the time goes:
time: 414 us; the launch traced here: 413 us
  waiting for transfers between devices  337 us (81%)
  local copies, waits for them, and re-layouts  32.7 us (8%)
  matrix products  16.7 us (4%)
  between operations  13.4 us (3%)
  other arithmetic  12.8 us (3%)
    all_gather x1, waiting for transfers between devices, per_device(): lax.all_gather(prefix_hidden, 'tensor', axis=2, tiled=True)  122 us
    all_gather x1, waiting for transfers between devices, per_device(): every_block = lax.all_gather(prefix_block, 'prompt', axis=0, tiled=True)  88.2 us
    reduce_scatter x1, waiting for transfers between devices, per_device(): lax.psum_scatter(terms.astype(jnp.bfloat16), 'tensor', scatter_dimension=...  80.5 us
    all_gather x1, waiting for transfers between devices, per_device(): lax.all_gather(state_hidden, 'tensor', axis=2, tiled=True)  45.2 us
    all_gather x1, local copies, waits for them, and re-layouts, per_device(): every_block = lax.all_gather(prefix_block, 'prompt', axis=0, tiled=True)  22.3 us
  transfers between devices with their start and end apart: 4, of which 4 were waited for; matrix products, arithmetic and copies ran while one was open for 6% of the time, Pallas kernels for 0%

commit v1 on v0

v1 whole, which is shorter than its diff:
```python
import functools

import jax
import jax.numpy as jnp
from jax import lax
from jax.experimental import pallas as pl
from jax.experimental.pallas import tpu as pltpu
from jax.sharding import Mesh, PartitionSpec as P

HEAD_DIM = 128
CHIPS = ("xl", "z")
TENSOR = ("xh", "y")
PROMPT = ("xl", "z", "c")
F32 = jnp.float32
BF16 = jnp.bfloat16


def vmem():
    return pl.BlockSpec(memory_space=pltpu.VMEM)


def smem():
    return pl.BlockSpec(memory_space=pltpu.SMEM)


def params(mib):
    return pltpu.CompilerParams(vmem_limit_bytes=mib << 20)


def inverse_rms(total, width):
    return lax.rsqrt(total / width + 1e-05)


def dot(a, b):
    return jnp.dot(a, b, preferred_element_type=F32)


def dot_t(a, b):
    return lax.dot_general(a, b, (((1,), (1,)), ((), ())), preferred_element_type=F32)


def prefix_kernel(where, gain, *refs):
    blocks, (w_k, w_v, w_a, w_b, own, back, acc) = refs[:8], refs[8:]
    xh, y, c = where[0], where[1], where[2]
    rows, part = blocks[0].shape
    tile = 256

    def step(r, carry):
        at = pl.ds(pl.multiple_of(r * tile, tile), tile)
        total = jnp.zeros((tile, 1), F32)
        for block in blocks:
            x = block[at, :].astype(F32)
            total += jnp.sum(x * x, axis=1, keepdims=True)
        scale = inverse_rms(total, 8 * part)
        for k, block in enumerate(blocks):
            half = xh if k < 4 else 1 - xh
            feature = half * 4 + ((y + 4 - k % 4) & 3)
            g = gain[feature].astype(F32)
            n = (block[at, :].astype(F32) * scale * g).astype(BF16)
            wat = pl.ds(pl.multiple_of(feature * part, part), part)
            w = jnp.concatenate([w_k[wat, :], w_v[wat, :], w_a[wat, :], w_b[wat, :]], axis=1)
            if k == 0:
                acc[...] = dot(n, w)
            else:
                acc[...] += dot(n, w)
        own[at, :] = acc[:, : 2 * HEAD_DIM].astype(BF16)
        a = acc[:, 2 * HEAD_DIM : 3 * HEAD_DIM]
        b = acc[:, 3 * HEAD_DIM :]
        back[at, :HEAD_DIM] = jnp.where(c == 0, a, b).astype(BF16)
        back[at, HEAD_DIM:] = jnp.where(c == 0, b, a).astype(BF16)
        return carry

    lax.fori_loop(0, rows // tile, step, 0)


def state_kernel(x, gain, w_q, w_k, w_v, q, k, v, acc):
    parts, rows, part = x.shape
    total = jnp.zeros((rows, 1), F32)
    for f in range(parts):
        h = x[f].astype(F32)
        total += jnp.sum(h * h, axis=1, keepdims=True)
    scale = inverse_rms(total, parts * part)
    for f in range(parts):
        n = (x[f].astype(F32) * scale * gain[f].astype(F32)).astype(BF16)
        at = slice(f * part, (f + 1) * part)
        w = jnp.concatenate([w_q[at, :], w_k[at, :], w_v[at, :]], axis=1)
        if f == 0:
            acc[...] = dot(n, w)
        else:
            acc[...] += dot(n, w)
    split = w_q.shape[1]
    q[...] = (acc[:, :split] * HEAD_DIM ** (-0.5)).astype(BF16)
    k[...] = acc[:, split : split + HEAD_DIM].astype(BF16)
    v[...] = acc[:, split + HEAD_DIM :].astype(BF16)


def attention_kernel(where, q, near, far, k, v, meta, w_out, out, att):
    xh, limit = where[0], where[1]
    rows = q.shape[0]
    half = near.shape[0]
    column = lax.broadcasted_iota(jnp.int32, (1, half), 1)
    near_ok = xh * half + column < limit
    far_ok = (1 - xh) * half + column < limit
    pick = (lax.broadcasted_iota(jnp.int32, (8, HEAD_DIM), 1) == 1).astype(BF16)
    present = dot_t(pick, meta[...])[0:1, :] > 0.5
    a = lax.broadcasted_iota(jnp.int32, (rows, rows), 0)
    b = lax.broadcasted_iota(jnp.int32, (rows, rows), 1)
    same = ((a >> 3) & 1) == ((b >> 3) & 1)
    before = (((b >> 4) << 3) | (b & 7)) <= (((a >> 4) << 3) | (a & 7))
    own_ok = same & before & present
    k_near, v_near = near[:, :HEAD_DIM], near[:, HEAD_DIM:]
    k_far, v_far = far[:, :HEAD_DIM], far[:, HEAD_DIM:]
    for h in range(q.shape[1] // HEAD_DIM):
        at = slice(h * HEAD_DIM, (h + 1) * HEAD_DIM)
        qh = q[:, at]
        s0 = jnp.where(near_ok, dot_t(qh, k_near), -1e30)
        s1 = jnp.where(far_ok, dot_t(qh, k_far), -1e30)
        s2 = jnp.where(own_ok, dot_t(qh, k[...]), -1e30)
        top = jnp.maximum(
            jnp.maximum(jnp.max(s0, axis=1, keepdims=True), jnp.max(s1, axis=1, keepdims=True)),
            jnp.max(s2, axis=1, keepdims=True),
        )
        p0 = jnp.where(near_ok, jnp.exp(s0 - top), 0.0)
        p1 = jnp.where(far_ok, jnp.exp(s1 - top), 0.0)
        p2 = jnp.where(own_ok, jnp.exp(s2 - top), 0.0)
        denom = (
            jnp.sum(p0, axis=1, keepdims=True)
            + jnp.sum(p1, axis=1, keepdims=True)
            + jnp.sum(p2, axis=1, keepdims=True)
        )
        numer = dot(p0.astype(BF16), v_near) + dot(p1.astype(BF16), v_far)
        numer += dot(p2.astype(BF16), v[...])
        att[:, at] = (numer / denom).astype(BF16)
    part = out.shape[2]

    def project(t, carry):
        at = pl.ds(pl.multiple_of(t * part, part), part)
        out[t] = dot(att[...], w_out[:, at]).astype(BF16)
        return carry

    lax.fori_loop(0, out.shape[0], project, 0)


def select_kernel(index, own, other, out):
    chips, slots = out.shape[:2]
    for q in range(chips):
        for s in range(slots):
            j = index[q, s]
            at = j & (chips - 1)
            out[q, s] = jnp.where(j < chips, own[at, s], other[at, s])


def select(index, own, other):
    return pl.pallas_call(
        select_kernel,
        out_shape=jax.ShapeDtypeStruct(own.shape, own.dtype),
        in_specs=[smem(), vmem(), vmem()],
        out_specs=vmem(),
        compiler_params=params(16),
        cost_estimate=pl.CostEstimate(flops=0, bytes_accessed=3 * own.size * 2, transcendentals=0),
        name="select_blocks",
    )(index, own, other)


def swap(x, axis):
    return lax.ppermute(x, axis, [(0, 1), (1, 0)])


def turn(x, s):
    return lax.ppermute(x, "y", [(i, (i + s) % 4) for i in range(4)])


def spread(x, axis):
    return lax.all_to_all(x, axis, 0, 0, tiled=True)


def per_device(
    state_hidden,
    prefix_hidden,
    norm_gain,
    w_query,
    w_key,
    w_value,
    w_out,
    scored_prompt,
    prefix_len,
    state_mask,
):
    xl, z, c = lax.axis_index("xl"), lax.axis_index("z"), lax.axis_index("c")
    xh, y = lax.axis_index("xh"), lax.axis_index("y")
    slots, length, part = state_hidden.shape
    parts = 8
    chips = 16
    piece = length // chips
    rows = slots * length
    half = prefix_hidden.shape[1] // 2
    gain = norm_gain.reshape(parts, 1, part)

    mine = lax.dynamic_slice_in_dim(prefix_hidden[0], xh * half, half)
    send = lax.dynamic_slice_in_dim(prefix_hidden[0], (1 - xh) * half, half)
    got = swap(send, "xh")
    w_a = swap(jnp.where(c == 0, w_key, w_value), "xh")
    w_b = swap(w_a, "c")
    blocks = [mine] + [turn(mine, s) for s in (1, 2, 3)]
    blocks += [got] + [turn(got, s) for s in (1, 2, 3)]

    lane = lax.broadcasted_iota(jnp.int32, (slots, length, HEAD_DIM), 2)
    meta = jnp.where(lane == 0, scored_prompt[0][:, None, None], state_mask[:, :, None])
    meta = jnp.where(lane < 2, meta, 0).astype(BF16)
    packed = jnp.concatenate([state_hidden, meta], axis=2)
    packed = packed.reshape(slots, chips, piece, part + HEAD_DIM).transpose(1, 0, 2, 3)
    here = spread(packed, CHIPS)
    there = swap(here, "c")
    ids = here[:, :, 0, part].astype(jnp.int32)
    ids_there = there[:, :, 0, part].astype(jnp.int32)
    chip = jnp.arange(chips, dtype=jnp.int32)
    wanted = (2 * chip + c)[:, None, None]
    inward = jnp.sum(
        jnp.where(ids[None] == wanted, chip[None, :, None], 0)
        + jnp.where(ids_there[None] == wanted, chips + chip[None, :, None], 0),
        axis=1,
    ).astype(jnp.int32)
    outward = jnp.where(ids % 2 == c, ids // 2, chips + ids // 2)
    routed = spread(select(inward, here, there), CHIPS).reshape(rows, part + HEAD_DIM)

    wide = jnp.broadcast_to(routed[None, :, :part], (parts, rows, part))
    wide = spread(wide, TENSOR)
    q, k, v = pl.pallas_call(
        state_kernel,
        out_shape=[
            jax.ShapeDtypeStruct((rows, w_query.shape[1]), BF16),
            jax.ShapeDtypeStruct((rows, HEAD_DIM), BF16),
            jax.ShapeDtypeStruct((rows, HEAD_DIM), BF16),
        ],
        in_specs=[vmem()] * 5,
        out_specs=[vmem()] * 3,
        scratch_shapes=[pltpu.VMEM((rows, w_query.shape[1] + 2 * HEAD_DIM), F32)],
        compiler_params=params(24),
        cost_estimate=pl.CostEstimate(flops=1610612736, bytes_accessed=8 << 20, transcendentals=0),
        name="state_projection",
    )(wide, gain, w_query, w_key, w_value)

    place = jnp.stack([xh, y, c]).astype(jnp.int32)
    near, back = pl.pallas_call(
        prefix_kernel,
        out_shape=[jax.ShapeDtypeStruct((half, 2 * HEAD_DIM), BF16)] * 2,
        in_specs=[smem()] + [vmem()] * 13,
        out_specs=[vmem()] * 2,
        scratch_shapes=[pltpu.VMEM((256, 4 * HEAD_DIM), F32)],
        compiler_params=params(24),
        cost_estimate=pl.CostEstimate(flops=2147483648, bytes_accessed=8 << 20, transcendentals=0),
        name="prefix_projection",
    )(place, gain, *blocks, w_key, w_value, w_a, w_b)
    far = swap(back, "xh")

    limit = lax.dynamic_index_in_dim(prefix_len, (xl * 8 + z) * 2 + c, keepdims=False)
    terms = pl.pallas_call(
        attention_kernel,
        out_shape=jax.ShapeDtypeStruct((parts, rows, part), BF16),
        in_specs=[smem()] + [vmem()] * 7,
        out_specs=vmem(),
        scratch_shapes=[pltpu.VMEM((rows, w_out.shape[0]), BF16)],
        compiler_params=params(32),
        cost_estimate=pl.CostEstimate(flops=1800000000, bytes_accessed=8 << 20, transcendentals=1310720),
        name="attention",
    )(jnp.stack([xh, limit]).astype(jnp.int32), q, near, far, k, v, routed[:, part:], w_out)

    mixed = jnp.sum(spread(terms, TENSOR).astype(F32), axis=0).astype(BF16)
    here = spread(mixed.reshape(chips, slots, piece, part), CHIPS)
    there = swap(here, "c")
    home = spread(select(outward, here, there), CHIPS)
    return home.transpose(1, 0, 2, 3).reshape(slots, length, part)


def solution(mesh):
    split = Mesh(mesh.devices.reshape(2, 8, 2, 2, 4), ("xl", "z", "c", "xh", "y"))
    placed = (
        P(PROMPT, None, TENSOR),
        P(PROMPT, None, TENSOR),
        P(),
        P(None, TENSOR),
        P(None, TENSOR),
        P(None, TENSOR),
        P(TENSOR, None),
        P(PROMPT, None),
        P(),
        P(PROMPT, None),
    )
    return jax.shard_map(
        per_device,
        mesh=split,
        in_specs=placed,
        out_specs=P(PROMPT, None, TENSOR),
        check_vma=False,
    )
```

time: 414 us -> 215 us (0.52)
  waiting for transfers between devices: 337 us -> 74 us
  blocking collectives: 0 us -> 63.3 us
  starting transfers between devices: 0.3 us -> 42.9 us
  local copies, waits for them, and re-layouts: 32.7 us -> 11.3 us
  Pallas kernels: 0 us -> 18 us
  matrix products: 16.7 us -> 0 us
  between operations: 13.4 us -> 0.16 us
  other arithmetic: 12.8 us -> 5.13 us
    all_gather x3 -> x0, waiting for transfers between devices: 255 us -> none  [the longest x1 122 us: per_device(): lax.all_gather(prefix_hidden, 'tensor', axis=2, tiled=True)]
    reduce_scatter x1 -> x0, waiting for transfers between devices: 80.5 us -> none  [per_device(): lax.psum_scatter(terms.astype(jnp.bfloat16), 'tensor', scatter_dimension=...]
    all_to_all x0 -> x3, blocking collectives: none -> 63.3 us  [spread(): return lax.all_to_all(x, axis, 0, 0, tiled=True)]
    ppermute x0 -> x12, waiting for transfers between devices: none -> 55.1 us  [the longest x6 36.1 us: swap(): return lax.ppermute(x, axis, [(0, 1), (1, 0)])]
    all_gather x1 -> x0, local copies, waits for them, and re-layouts: 22.3 us -> none  [per_device(): every_block = lax.all_gather(prefix_block, 'prompt', axis=0, tiled=True)]
    ppermute x0 -> x12, starting transfers between devices: none -> 21.9 us  [the longest x6 12.7 us: turn(): return lax.ppermute(x, 'y', [(i, (i + s) % 4) for i in range(4)])]
    all_to_all x0 -> x3, starting transfers between devices: none -> 21 us  [spread(): return lax.all_to_all(x, axis, 0, 0, tiled=True)]
    all_to_all x0 -> x3, waiting for transfers between devices: none -> 19 us  [spread(): return lax.all_to_all(x, axis, 0, 0, tiled=True)]
  transfers between devices with their start and end apart: 4 -> 15, of which waited for: 4 -> 9; matrix products, arithmetic and copies ran while one was open for 6% -> 3% of each run, Pallas kernels for 0% -> 5%
where the time goes in v1:
time: 215 us
  waiting for transfers between devices  74 us (34%)
  blocking collectives  63.3 us (29%)
  starting transfers between devices  42.9 us (20%)
  Pallas kernels  18 us (8%)
  local copies, waits for them, and re-layouts  11.3 us (5%)
  other arithmetic  5.13 us (2%)
    all_to_all x3, blocking collectives, spread(): return lax.all_to_all(x, axis, 0, 0, tiled=True)  63.3 us
    ppermute x6, waiting for transfers between devices, swap(): return lax.ppermute(x, axis, [(0, 1), (1, 0)])  36.1 us
    all_to_all x3, starting transfers between devices, spread(): return lax.all_to_all(x, axis, 0, 0, tiled=True)  21 us
    all_to_all x3, waiting for transfers between devices, spread(): return lax.all_to_all(x, axis, 0, 0, tiled=True)  19 us
    ppermute x6, waiting for transfers between devices, turn(): return lax.ppermute(x, 'y', [(i, (i + s) % 4) for i in range(4)])  18.9 us
    ppermute x6, starting transfers between devices, turn(): return lax.ppermute(x, 'y', [(i, (i + s) % 4) for i in range(4)])  12.7 us
    ppermute x6, starting transfers between devices, swap(): return lax.ppermute(x, axis, [(0, 1), (1, 0)])  9.17 us
    pallas_call x1, Pallas kernels, per_device(): pl.pallas_call(prefix_kernel, out_shape=[jax.ShapeDtypeStruct((half, 2 *...  6.23 us
  transfers between devices with their start and end apart: 15, of which 9 were waited for; matrix products, arithmetic and copies ran while one was open for 3% of the time, Pallas kernels for 5%

profile of v1, /device:TPU:32, one launch (start us, length us, event | category | flops | bytes accessed | tf_op | source)
XLA Modules:
  0.0 214.8 jit_solution(9334923169879721599)
XLA Ops:
  1.0 1.7 copy_bitcast_fusion
  2.7 9.5 %all-to-all-start = ((bf16[16,2,8,640]{3,2,1,0:T(8,128)(2,1)}), bf16[16,2,8,640]{3,2,1,0:T(8,128)(2,1)S(1)}, u32[]{:S(2)}, u32[]{:S(2)}) async-start(bf16[16,2,8,640]{3,2,1,0:T(8,128)(2,1)} %copy_bitcast_fusion), calls=%async_computation | async-start | bytes 655360 | tf_op jit(solution)/shard_map/all_to_all | solution.py:174
  12.2 11.2 %all-to-all-done.own = bf16[16,2,8,640]{3,2,1,0:T(8,128)(2,1)S(1)} async-done(((bf16[16,2,8,640]{3,2,1,0:T(8,128)(2,1)}), bf16[16,2,8,640]{3,2,1,0:T(8,128)(2,1)S(1)}, u32[]{:S(2)}, u32[]{:S(2)}) %all-to-all-start) | async-done | bytes 327712 | tf_op jit(solution)/shard_map/all_to_all | solution.py:174
  26.9 4.8 %all-to-all-start.1 = ((bf16[16,2,8,640]{3,2,1,0:T(8,128)(2,1)}), bf16[16,2,8,640]{3,2,1,0:T(8,128)(2,1)S(1)}, u32[]{:S(2)}, u32[]{:S(2)}) async-start(bf16[16,2,8,640]{3,2,1,0:T(8,128)(2,1)} %select_blocks.2), calls=%async_computation.1 | async-start | bytes 655360 | tf_op jit(solution)/shard_map/all_to_all | solution.py:174
  32.8 2.7 %collective-permute-start.8 = (bf16[4096,128]{1,0:T(8,128)(2,1)}, bf16[4096,128]{1,0:T(8,128)(2,1)}, u32[]{:S(2)}, u32[]{:S(2)}) collective-permute-start(bf16[4096,128]{1,0:T(8,128)(2,1)} %broadcast_select_fusion), channel_id=1, source_target_pairs={{0,4},{4,0},{1,5},{5,1},{2,6},{6,2},{3,7},{7,3},{8,12},{12,8},{9,1... | collective-permute-start | bytes 3145736 | tf_op jit(solution)/shard_map/ppermute | solution.py:166
  35.5 7.8 %all-to-all-done.1 = bf16[16,2,8,640]{3,2,1,0:T(8,128)(2,1)S(1)} async-done(((bf16[16,2,8,640]{3,2,1,0:T(8,128)(2,1)}), bf16[16,2,8,640]{3,2,1,0:T(8,128)(2,1)S(1)}, u32[]{:S(2)}, u32[]{:S(2)}) %all-to-all-start.1) | async-done | bytes 327712 | tf_op jit(solution)/shard_map/all_to_all | solution.py:174
  44.8 6.6 %all-to-all-start.2 = ((bf16[8,256,512]{2,1,0:T(8,128)(2,1)}), bf16[8,256,512]{2,1,0:T(8,128)(2,1)}, u32[]{:S(2)}, u32[]{:S(2)}) async-start(bf16[8,256,512]{2,1,0:T(8,128)(2,1)} %broadcast_in_dim.56), calls=%async_computation.2 | async-start | bytes 4194304 | tf_op jit(solution)/shard_map/all_to_all | solution.py:174
  52.8 3.6 %collective-permute-start.4 = (bf16[512,512]{1,0:T(8,128)(2,1)S(1)}, bf16[512,512]{1,0:T(8,128)(2,1)S(1)}, u32[]{:S(2)}, u32[]{:S(2)}) collective-permute-start(bf16[512,512]{1,0:T(8,128)(2,1)S(1)} %get-tuple-element.15), channel_id=1, source_target_pairs={{0,4},{4,0},{1,5},{5,1},{2,6},{6,2},{3,7},{7,3},{8,12},{12,8},{9,1... | collective-permute-start | bytes 1572872 | tf_op jit(solution)/shard_map/ppermute | solution.py:166
  57.8 2.7 %collective-permute-start.2 = (bf16[512,512]{1,0:T(8,128)(2,1)S(1)}, bf16[512,512]{1,0:T(8,128)(2,1)S(1)}, u32[]{:S(2)}, u32[]{:S(2)}) collective-permute-start(bf16[512,512]{1,0:T(8,128)(2,1)S(1)} %get-tuple-element.16.refs_0_), channel_id=1, source_target_pairs={{0,2},{1,3},{2,0},{3,1},{4,6},{5,7},{6,4},{7,5},{8,10},{9,11},{10,... | collective-permute-start | bytes 1572872 | tf_op jit(solution)/shard_map/ppermute | solution.py:170
  60.5 2.6 %collective-permute-done.8.refs_10_ = bf16[4096,128]{1,0:T(8,128)(2,1)} collective-permute-done((bf16[4096,128]{1,0:T(8,128)(2,1)}, bf16[4096,128]{1,0:T(8,128)(2,1)}, u32[]{:S(2)}, u32[]{:S(2)}) %collective-permute-start.8) | collective-permute-done | bytes 1048608 | tf_op jit(solution)/shard_map/ppermute | solution.py:166
  63.1 3.0 %collective-permute-start.3 = (bf16[512,512]{1,0:T(8,128)(2,1)S(1)}, bf16[512,512]{1,0:T(8,128)(2,1)}, u32[]{:S(2)}, u32[]{:S(2)}) collective-permute-start(bf16[512,512]{1,0:T(8,128)(2,1)S(1)} %get-tuple-element.16.refs_0_), channel_id=1, source_target_pairs={{0,3},{1,0},{2,1},{3,2},{4,7},{5,4},{6,5},{7,6},{8,11},{9,8},{10,9... | collective-permute-start | bytes 1572872 | tf_op jit(solution)/shard_map/ppermute | solution.py:170
  66.1 30.6 %collective-permute-done.4.refs_4_ = bf16[512,512]{1,0:T(8,128)(2,1)S(1)} collective-permute-done((bf16[512,512]{1,0:T(8,128)(2,1)S(1)}, bf16[512,512]{1,0:T(8,128)(2,1)S(1)}, u32[]{:S(2)}, u32[]{:S(2)}) %collective-permute-start.4) | collective-permute-done | bytes 524320 | tf_op jit(solution)/shard_map/ppermute | solution.py:166
  96.7 1.5 collective-permute-start.5
  99.1 2.9 %collective-permute-start.6 = (bf16[512,512]{1,0:T(8,128)(2,1)S(1)}, bf16[512,512]{1,0:T(8,128)(2,1)}, u32[]{:S(2)}, u32[]{:S(2)}) collective-permute-start(bf16[512,512]{1,0:T(8,128)(2,1)S(1)} %collective-permute-done.4.refs_4_), channel_id=1, source_target_pairs={{0,2},{1,3},{2,0},{3,1},{4,6},{5,7},{6,4},{7,5},{8,10},{9,11},{10,... | collective-permute-start | bytes 1572872 | tf_op jit(solution)/shard_map/ppermute | solution.py:170
  104.7 7.1 %collective-permute-done.5.refs_5_ = bf16[512,512]{1,0:T(8,128)(2,1)} collective-permute-done((bf16[512,512]{1,0:T(8,128)(2,1)S(1)}, bf16[512,512]{1,0:T(8,128)(2,1)}, u32[]{:S(2)}, u32[]{:S(2)}) %collective-permute-start.5) | collective-permute-done | bytes 524320 | tf_op jit(solution)/shard_map/ppermute | solution.py:170
  111.7 11.5 %collective-permute-done.6.refs_6_ = bf16[512,512]{1,0:T(8,128)(2,1)} collective-permute-done((bf16[512,512]{1,0:T(8,128)(2,1)S(1)}, bf16[512,512]{1,0:T(8,128)(2,1)}, u32[]{:S(2)}, u32[]{:S(2)}) %collective-permute-start.6) | collective-permute-done | bytes 524320 | tf_op jit(solution)/shard_map/ppermute | solution.py:170
  125.7 6.2 %prefix_projection.1 = (bf16[512,256]{1,0:T(8,128)(2,1)S(1)}, bf16[512,256]{1,0:T(8,128)(2,1)}) custom-call(s32[3]{0:T(128)S(1)} %pad_add_fusion.1.where, bf16[8,1,512]{2,1,0:T(2,128)(2,1)S(1)} %reshape.51.gain, bf16[512,512]{1,0:T(8,128)(2,1)S(1)} %get-tuple-element.16.refs_0_, bf16[512,512]{1,0:T(8,128)(2,1)S(1)} %copy-done.5, ...), custom_call_target="tpu_custom_call" | custom-call | flops 2147483648 | bytes 8388608 | tf_op jit(solution)/shard_map/prefix_projection/pallas_call | solution.py:244
  131.9 2.8 %collective-permute-start.10 = (bf16[512,256]{1,0:T(8,128)(2,1)}, bf16[512,256]{1,0:T(8,128)(2,1)S(1)}, u32[]{:S(2)}, u32[]{:S(2)}) collective-permute-start(bf16[512,256]{1,0:T(8,128)(2,1)} %get-tuple-element.12), channel_id=1, source_target_pairs={{0,4},{4,0},{1,5},{5,1},{2,6},{6,2},{3,7},{7,3},{8,12},{12,8},{9,1... | collective-permute-start | bytes 786440 | tf_op jit(solution)/shard_map/ppermute | solution.py:166
  136.3 2.2 %copy-done.3 = bf16[4096,512]{1,0:T(8,128)(2,1)S(1)} copy-done((bf16[4096,512]{1,0:T(8,128)(2,1)S(1)}, bf16[4096,512]{1,0:T(8,128)(2,1)}, u32[]{:S(2)}) %copy-start.3) | copy-done | bytes 4194328
  138.5 4.0 %state_projection.1 = (bf16[256,512]{1,0:T(8,128)(2,1)S(1)}, bf16[256,128]{1,0:T(8,128)(2,1)S(1)}, bf16[256,128]{1,0:T(8,128)(2,1)S(1)}) custom-call(bf16[8,256,512]{2,1,0:T(8,128)(2,1)} %all-to-all-done.2.x, bf16[8,1,512]{2,1,0:T(2,128)(2,1)S(1)} %reshape.51.gain, bf16[4096,512]{1,0:T(8,128)(2,1)S(1)} %copy-done.3, bf16[4096,128]{1,0:T(8,128)(2,1)S(1)} %copy-done, ...), custom_call_target="tpu_custom_call" | custom-call | flops 1610612736 | bytes 8388608 | tf_op jit(solution)/shard_map/state_projection/pallas_call | solution.py:228
  142.5 5.6 %attention.1 = bf16[8,256,512]{2,1,0:T(8,128)(2,1)S(1)} custom-call(s32[2]{0:T(128)S(1)} %pad_add_fusion.where, bf16[256,512]{1,0:T(8,128)(2,1)S(1)} %get-tuple-element.10.q, bf16[512,256]{1,0:T(8,128)(2,1)S(1)} %get-tuple-element.11.near, bf16[512,256]{1,0:T(8,128)(2,1)S(1)} %collective-permute-done.10.far, bf16[256,128]{1,0:T(8,128)(2,1)S(1)} %get-tuple-element.13.k, ...), custom_call_target="tpu_custom_call" | custom-call | flops 1800000000 | bytes 8388608 | tf_op jit(solution)/shard_map/attention/pallas_call | solution.py:257
  148.1 33.1 %all_to_all.30 = bf16[8,256,512]{2,1,0:T(8,128)(2,1)S(1)} all-to-all(bf16[8,256,512]{2,1,0:T(8,128)(2,1)S(1)} %attention.1), channel_id=1, replica_groups=mesh['xl'=2,'z'=8,'c'=2,'xh'=2,'y'=4] {'xh','y'}, dimensions={0} | all-to-all | bytes 4194304 | tf_op jit(solution)/shard_map/all_to_all | solution.py:174
  181.5 15.9 %all_to_all.31.own = bf16[16,2,8,512]{3,2,1,0:T(8,128)(2,1)S(1)} all-to-all(bf16[16,2,8,512]{3,2,1,0:T(8,128)(2,1)S(1)} %bitcast.24), channel_id=1, replica_groups=mesh['xl'=2,'z'=8,'c'=2,'xh'=2,'y'=4] {'xl','z'}, dimensions={0} | all-to-all | bytes 524288 | tf_op jit(solution)/shard_map/all_to_all | solution.py:174
  199.7 14.4 %all_to_all.32 = bf16[16,2,8,512]{3,2,1,0:T(8,128)(2,1)S(1)} all-to-all(bf16[16,2,8,512]{3,2,1,0:T(8,128)(2,1)S(1)} %select_blocks.3), channel_id=1, replica_groups=mesh['xl'=2,'z'=8,'c'=2,'xh'=2,'y'=4] {'xl','z'}, dimensions={0} | all-to-all | bytes 524288 | tf_op jit(solution)/shard_map/all_to_all | solution.py:174
  (60 shorter events, 20.6 us)
Async XLA Ops:
  0.0 31.7 %copy-start = (bf16[4096,128]{1,0:T(8,128)(2,1)S(1)}, bf16[4096,128]{1,0:T(8,128)(2,1)}, u32[]{:S(2)}) copy-start(bf16[4096,128]{1,0:T(8,128)(2,1)} %refs_8_.1) | copy-start | bytes 3145732
  0.0 31.7 %copy-start.1 = (bf16[4096,128]{1,0:T(8,128)(2,1)S(1)}, bf16[4096,128]{1,0:T(8,128)(2,1)}, u32[]{:S(2)}) copy-start(bf16[4096,128]{1,0:T(8,128)(2,1)} %refs_9_.1) | copy-start | bytes 3145732
  2.7 20.7 %all-to-all-start = ((bf16[16,2,8,640]{3,2,1,0:T(8,128)(2,1)}), bf16[16,2,8,640]{3,2,1,0:T(8,128)(2,1)S(1)}, u32[]{:S(2)}, u32[]{:S(2)}) async-start(bf16[16,2,8,640]{3,2,1,0:T(8,128)(2,1)} %copy_bitcast_fusion), calls=%async_computation | async-start | bytes 655360 | tf_op jit(solution)/shard_map/all_to_all | solution.py:174
  23.4 1.6 collective-permute-start
  26.9 16.5 %all-to-all-start.1 = ((bf16[16,2,8,640]{3,2,1,0:T(8,128)(2,1)}), bf16[16,2,8,640]{3,2,1,0:T(8,128)(2,1)S(1)}, u32[]{:S(2)}, u32[]{:S(2)}) async-start(bf16[16,2,8,640]{3,2,1,0:T(8,128)(2,1)} %select_blocks.2), calls=%async_computation.1 | async-start | bytes 655360 | tf_op jit(solution)/shard_map/all_to_all | solution.py:174
  32.8 30.3 %collective-permute-start.8 = (bf16[4096,128]{1,0:T(8,128)(2,1)}, bf16[4096,128]{1,0:T(8,128)(2,1)}, u32[]{:S(2)}, u32[]{:S(2)}) collective-permute-start(bf16[4096,128]{1,0:T(8,128)(2,1)} %broadcast_select_fusion), channel_id=1, source_target_pairs={{0,4},{4,0},{1,5},{5,1},{2,6},{6,2},{3,7},{7,3},{8,12},{12,8},{9,1... | collective-permute-start | bytes 3145736 | tf_op jit(solution)/shard_map/ppermute | solution.py:166
  43.3 1.5 copy-start.8
  44.8 91.5 %all-to-all-start.2 = ((bf16[8,256,512]{2,1,0:T(8,128)(2,1)}), bf16[8,256,512]{2,1,0:T(8,128)(2,1)}, u32[]{:S(2)}, u32[]{:S(2)}) async-start(bf16[8,256,512]{2,1,0:T(8,128)(2,1)} %broadcast_in_dim.56), calls=%async_computation.2 | async-start | bytes 4194304 | tf_op jit(solution)/shard_map/all_to_all | solution.py:174
  51.5 52.5 %copy-start.9 = (bf16[4096]{0:T(1024)(128)(2,1)S(1)}, bf16[4096]{0:T(1024)(128)(2,1)}, u32[]{:S(2)}) copy-start(bf16[4096]{0:T(1024)(128)(2,1)} %param.12) | copy-start | bytes 24580
  51.5 52.5 %copy-start.10 = (s32[32]{0:T(128)S(1)}, s32[32]{0:T(128)}, u32[]{:S(2)}) copy-start(s32[32]{0:T(128)} %param.18) | copy-start | bytes 388
  52.8 44.0 %collective-permute-start.4 = (bf16[512,512]{1,0:T(8,128)(2,1)S(1)}, bf16[512,512]{1,0:T(8,128)(2,1)S(1)}, u32[]{:S(2)}, u32[]{:S(2)}) collective-permute-start(bf16[512,512]{1,0:T(8,128)(2,1)S(1)} %get-tuple-element.15), channel_id=1, source_target_pairs={{0,4},{4,0},{1,5},{5,1},{2,6},{6,2},{3,7},{7,3},{8,12},{12,8},{9,1... | collective-permute-start | bytes 1572872 | tf_op jit(solution)/shard_map/ppermute | solution.py:166
  56.4 41.9 %collective-permute-start.1 = (bf16[512,512]{1,0:T(8,128)(2,1)S(1)}, bf16[512,512]{1,0:T(8,128)(2,1)S(1)}, u32[]{:S(2)}, u32[]{:S(2)}) collective-permute-start(bf16[512,512]{1,0:T(8,128)(2,1)S(1)} %get-tuple-element.16.refs_0_), channel_id=1, source_target_pairs={{0,1},{1,2},{2,3},{3,0},{4,5},{5,6},{6,7},{7,4},{8,9},{9,10},{10,1... | collective-permute-start | bytes 1572872 | tf_op jit(solution)/shard_map/ppermute | solution.py:170
  57.8 44.2 %collective-permute-start.2 = (bf16[512,512]{1,0:T(8,128)(2,1)S(1)}, bf16[512,512]{1,0:T(8,128)(2,1)S(1)}, u32[]{:S(2)}, u32[]{:S(2)}) collective-permute-start(bf16[512,512]{1,0:T(8,128)(2,1)S(1)} %get-tuple-element.16.refs_0_), channel_id=1, source_target_pairs={{0,2},{1,3},{2,0},{3,1},{4,6},{5,7},{6,4},{7,5},{8,10},{9,11},{10,... | collective-permute-start | bytes 1572872 | tf_op jit(solution)/shard_map/ppermute | solution.py:170
  63.1 60.5 %collective-permute-start.9 = (bf16[4096,128]{1,0:T(8,128)(2,1)}, bf16[4096,128]{1,0:T(8,128)(2,1)}, u32[]{:S(2)}, u32[]{:S(2)}) collective-permute-start(bf16[4096,128]{1,0:T(8,128)(2,1)} %collective-permute-done.8.refs_10_), channel_id=1, source_target_pairs={{0,8},{8,0},{1,9},{9,1},{2,10},{10,2},{3,11},{11,3},{4,12},{12,4},... | collective-permute-start | bytes 3145736 | tf_op jit(solution)/shard_map/ppermute | solution.py:166
  63.1 41.5 %collective-permute-start.3 = (bf16[512,512]{1,0:T(8,128)(2,1)S(1)}, bf16[512,512]{1,0:T(8,128)(2,1)}, u32[]{:S(2)}, u32[]{:S(2)}) collective-permute-start(bf16[512,512]{1,0:T(8,128)(2,1)S(1)} %get-tuple-element.16.refs_0_), channel_id=1, source_target_pairs={{0,3},{1,0},{2,1},{3,2},{4,7},{5,4},{6,5},{7,6},{8,11},{9,8},{10,9... | collective-permute-start | bytes 1572872 | tf_op jit(solution)/shard_map/ppermute | solution.py:170
  96.7 15.0 %collective-permute-start.5 = (bf16[512,512]{1,0:T(8,128)(2,1)S(1)}, bf16[512,512]{1,0:T(8,128)(2,1)}, u32[]{:S(2)}, u32[]{:S(2)}) collective-permute-start(bf16[512,512]{1,0:T(8,128)(2,1)S(1)} %collective-permute-done.4.refs_4_), channel_id=1, source_target_pairs={{0,1},{1,2},{2,3},{3,0},{4,5},{5,6},{6,7},{7,4},{8,9},{9,10},{10,1... | collective-permute-start | bytes 1572872 | tf_op jit(solution)/shard_map/ppermute | solution.py:170
  99.1 24.2 %collective-permute-start.6 = (bf16[512,512]{1,0:T(8,128)(2,1)S(1)}, bf16[512,512]{1,0:T(8,128)(2,1)}, u32[]{:S(2)}, u32[]{:S(2)}) collective-permute-start(bf16[512,512]{1,0:T(8,128)(2,1)S(1)} %collective-permute-done.4.refs_4_), channel_id=1, source_target_pairs={{0,2},{1,3},{2,0},{3,1},{4,6},{5,7},{6,4},{7,5},{8,10},{9,11},{10,... | collective-permute-start | bytes 1572872 | tf_op jit(solution)/shard_map/ppermute | solution.py:170
  102.8 20.8 %collective-permute-start.7 = (bf16[512,512]{1,0:T(8,128)(2,1)S(1)}, bf16[512,512]{1,0:T(8,128)(2,1)}, u32[]{:S(2)}, u32[]{:S(2)}) collective-permute-start(bf16[512,512]{1,0:T(8,128)(2,1)S(1)} %collective-permute-done.4.refs_4_), channel_id=1, source_target_pairs={{0,3},{1,0},{2,1},{3,2},{4,7},{5,4},{6,5},{7,6},{8,11},{9,8},{10,9... | collective-permute-start | bytes 1572872 | tf_op jit(solution)/shard_map/ppermute | solution.py:170
  123.6 1.0 copy-start.5
  124.6 1.0 copy-start.7
  131.9 10.5 %collective-permute-start.10 = (bf16[512,256]{1,0:T(8,128)(2,1)}, bf16[512,256]{1,0:T(8,128)(2,1)S(1)}, u32[]{:S(2)}, u32[]{:S(2)}) collective-permute-start(bf16[512,256]{1,0:T(8,128)(2,1)} %get-tuple-element.12), channel_id=1, source_target_pairs={{0,4},{4,0},{1,5},{5,1},{2,6},{6,2},{3,7},{7,3},{8,12},{12,8},{9,1... | collective-permute-start | bytes 786440 | tf_op jit(solution)/shard_map/ppermute | solution.py:166
  136.3 2.2 %copy-start.3 = (bf16[4096,512]{1,0:T(8,128)(2,1)S(1)}, bf16[4096,512]{1,0:T(8,128)(2,1)}, u32[]{:S(2)}) copy-start(bf16[4096,512]{1,0:T(8,128)(2,1)} %w_q.1) | copy-start | bytes 12582916
  138.5 4.0 %copy-start.2 = (bf16[512,4096]{1,0:T(8,128)(2,1)S(1)}, bf16[512,4096]{1,0:T(8,128)(2,1)}, u32[]{:S(2)}) copy-start(bf16[512,4096]{1,0:T(8,128)(2,1)} %w_out.1) | copy-start | bytes 12582916
  197.4 1.5 collective-permute-start.11
  (2 other events, 1.7 us)

commit v2 on v1

v2 whole, which is shorter than its diff:
```python
import functools

import jax
import jax.numpy as jnp
from jax import lax
from jax.experimental import pallas as pl
from jax.experimental.pallas import tpu as pltpu
from jax.sharding import Mesh, PartitionSpec as P

HEAD_DIM = 128
CHIPS = ("xl", "z")
TENSOR = ("xh", "y")
PROMPT = ("xl", "z", "c")
F32 = jnp.float32
BF16 = jnp.bfloat16


def vmem():
    return pl.BlockSpec(memory_space=pltpu.VMEM)


def smem():
    return pl.BlockSpec(memory_space=pltpu.SMEM)


def anywhere():
    return pl.BlockSpec(memory_space=pltpu.HBM)


def in_hbm(x):
    return pltpu.with_memory_space_constraint(x, pltpu.HBM)


def params(mib):
    return pltpu.CompilerParams(vmem_limit_bytes=mib << 20)


def inverse_rms(total, width):
    return lax.rsqrt(total / width + 1e-05)


def dot(a, b):
    return jnp.dot(a, b, preferred_element_type=F32)


def dot_t(a, b):
    return lax.dot_general(a, b, (((1,), (1,)), ((), ())), preferred_element_type=F32)


def to_row(column, eye):
    return jnp.sum(jnp.where(eye, column, 0.0), axis=0, keepdims=True)


def to_column(row, eye):
    return jnp.sum(jnp.where(eye, row, 0.0), axis=1, keepdims=True)


def unit(size):
    return lax.broadcasted_iota(jnp.int32, (size, size), 0) == lax.broadcasted_iota(jnp.int32, (size, size), 1)


def prefix_kernel(where, gain, *refs):
    blocks, weights, (own, back, squares, x, w, acc, x_sem, w_sem) = refs[:5], refs[5:9], refs[9:]
    xh, y, c = where[0], where[1], where[2]
    parts, rows, part = x.shape
    w_copies = []
    for k, b in enumerate(weights):
        source = b.at[pl.ds(pl.multiple_of(xh * parts * part, part), parts * part), :] if k < 2 else b
        w_copies.append(pltpu.make_async_copy(source, w.at[:, pl.ds(k * HEAD_DIM, HEAD_DIM)], w_sem.at[k]))
    middle = rows // 2
    places = [x.at[0], x.at[1], x.at[2, pl.ds(0, middle), :], x.at[2, pl.ds(middle, middle), :], x.at[3]]
    x_copies = [pltpu.make_async_copy(b, p, x_sem.at[k]) for k, (b, p) in enumerate(zip(blocks, places))]
    x_copies[0].start()
    for copy in w_copies + x_copies[1:]:
        copy.start()
    total = jnp.zeros((rows, 1), F32)
    for k in range(parts):
        for copy in ([x_copies[0]], [x_copies[1]], x_copies[2:4], [x_copies[4]])[k]:
            copy.wait()
        if k == 0:
            for copy in w_copies:
                copy.wait()
        feature = (y + parts - k) & (parts - 1)
        h = x[k].astype(F32)
        total += jnp.sum(h * h, axis=1, keepdims=True)
        n = (h * gain[xh * parts + feature].astype(F32)).astype(BF16)
        term = dot(n, w[pl.ds(pl.multiple_of(feature * part, part), part), :])
        if k == 0:
            acc[...] = term
        else:
            acc[...] += term
    own[...] = acc[:, : 2 * HEAD_DIM]
    a = acc[:, 2 * HEAD_DIM : 3 * HEAD_DIM].astype(BF16)
    b = acc[:, 3 * HEAD_DIM :].astype(BF16)
    back[:, :HEAD_DIM] = jnp.where(c == 0, a, b)
    back[:, HEAD_DIM:] = jnp.where(c == 0, b, a)
    eye = unit(HEAD_DIM)
    for r in range(rows // HEAD_DIM):
        squares[r : r + 1, :] = to_row(total[r * HEAD_DIM : (r + 1) * HEAD_DIM], eye)


def state_kernel(blocks, gain, w_q, w_k, w_v, q, k, v, x, w, acc, x_sem, w_sem):
    parts, rows, part = x.shape
    split = w_q.shape[1]
    x_copies = [pltpu.make_async_copy(blocks.at[f], x.at[f], x_sem.at[f]) for f in range(parts)]
    w_copies = []
    for f in range(parts):
        at = pl.ds(f * part, part)
        w_copies.append(
            [
                pltpu.make_async_copy(w_q.at[at, :], w.at[at, pl.ds(0, split)], w_sem.at[0, f]),
                pltpu.make_async_copy(w_k.at[at, :], w.at[at, pl.ds(split, HEAD_DIM)], w_sem.at[1, f]),
                pltpu.make_async_copy(w_v.at[at, :], w.at[at, pl.ds(split + HEAD_DIM, HEAD_DIM)], w_sem.at[2, f]),
            ]
        )
    for f in range(parts):
        x_copies[f].start()
        for copy in w_copies[f]:
            copy.start()
    total = jnp.zeros((rows, 1), F32)
    for f in range(parts):
        x_copies[f].wait()
        h = x[f].astype(F32)
        total += jnp.sum(h * h, axis=1, keepdims=True)
        n = (h * gain[f].astype(F32)).astype(BF16)
        for copy in w_copies[f]:
            copy.wait()
        term = dot(n, w[f * part : (f + 1) * part, :])
        if f == 0:
            acc[...] = term
        else:
            acc[...] += term
    scale = inverse_rms(total, parts * part)
    q[...] = (acc[:, :split] * (scale * HEAD_DIM ** (-0.5))).astype(BF16)
    k[...] = (acc[:, split : split + HEAD_DIM] * scale).astype(BF16)
    v[...] = (acc[:, split + HEAD_DIM :] * scale).astype(BF16)


def attention_kernel(limit, q, own, far, squares, far_squares, k, v, meta, w_out, out, att, kv):
    rows = q.shape[0]
    length = own.shape[0]
    eye = unit(HEAD_DIM)
    for r in range(length // HEAD_DIM):
        at = slice(r * HEAD_DIM, (r + 1) * HEAD_DIM)
        total = to_column(squares[r : r + 1, :] + far_squares[r : r + 1, :], eye)
        kv[at, :] = ((own[at, :] + far[at, :].astype(F32)) * inverse_rms(total, 4096)).astype(BF16)
    near_ok = lax.broadcasted_iota(jnp.int32, (1, length), 1) < limit[0]
    pick = (lax.broadcasted_iota(jnp.int32, (8, HEAD_DIM), 1) == 1).astype(BF16)
    present = dot_t(pick, meta[...])[0:1, :] > 0.5
    a = lax.broadcasted_iota(jnp.int32, (rows, rows), 0)
    b = lax.broadcasted_iota(jnp.int32, (rows, rows), 1)
    same = ((a >> 3) & 1) == ((b >> 3) & 1)
    before = (((b >> 4) << 3) | (b & 7)) <= (((a >> 4) << 3) | (a & 7))
    own_ok = same & before & present
    for h in range(q.shape[1] // HEAD_DIM):
        at = slice(h * HEAD_DIM, (h + 1) * HEAD_DIM)
        qh = q[:, at]
        s0 = jnp.where(near_ok, dot_t(qh, kv[:, :HEAD_DIM]), -1e30)
        s1 = jnp.where(own_ok, dot_t(qh, k[...]), -1e30)
        top = jnp.maximum(jnp.max(s0, axis=1, keepdims=True), jnp.max(s1, axis=1, keepdims=True))
        p0 = jnp.where(near_ok, jnp.exp(s0 - top), 0.0)
        p1 = jnp.where(own_ok, jnp.exp(s1 - top), 0.0)
        denom = jnp.sum(p0, axis=1, keepdims=True) + jnp.sum(p1, axis=1, keepdims=True)
        numer = dot(p0.astype(BF16), kv[:, HEAD_DIM:]) + dot(p1.astype(BF16), v[...])
        att[:, at] = (numer / denom).astype(BF16)
    part = out.shape[2]

    def project(t, carry):
        at = pl.ds(pl.multiple_of(t * part, part), part)
        out[t] = dot(att[...], w_out[:, at]).astype(BF16)
        return carry

    lax.fori_loop(0, out.shape[0], project, 0)


def select_kernel(index, own, other, *rest):
    out = rest[-1]
    chips, slots = out.shape[:2]
    for q in range(chips):
        for s in range(slots):
            j = index[q, s]
            at = j & (chips - 1)
            out[q, s] = jnp.where(j < chips, own[at, s], other[at, s])


def repeat_kernel(x, *rest):
    out = rest[-1]
    for t in range(out.shape[0]):
        out[t] = x[:, : out.shape[2]]


def repeat(x, parts, part, after):
    return pl.pallas_call(
        repeat_kernel,
        out_shape=jax.ShapeDtypeStruct((parts, x.shape[0], part), x.dtype),
        in_specs=[vmem()] + [anywhere()] * len(after),
        out_specs=vmem(),
        compiler_params=params(6),
        cost_estimate=pl.CostEstimate(flops=0, bytes_accessed=2 << 20, transcendentals=0),
        name="repeat_rows",
    )(x, *after)


def select(index, own, other, after=()):
    return pl.pallas_call(
        select_kernel,
        out_shape=jax.ShapeDtypeStruct(own.shape, own.dtype),
        in_specs=[smem(), vmem(), vmem()] + [anywhere()] * len(after),
        out_specs=vmem(),
        compiler_params=params(6),
        cost_estimate=pl.CostEstimate(flops=0, bytes_accessed=3 * own.size * 2, transcendentals=0),
        name="select_blocks",
    )(index, own, other, *after)


def swap(x, axis):
    return lax.ppermute(x, axis, [(0, 1), (1, 0)])


def turn(x, s):
    return lax.ppermute(x, "y", [(i, (i + s) % 4) for i in range(4)])


def spread(x, axis):
    return lax.all_to_all(x, axis, 0, 0, tiled=True)


def blocking(lengths, x, axis):
    return lax.cond(lengths[0] > -1, lambda p: spread(p, axis), lambda p: p, x)


def per_device(
    state_hidden,
    prefix_hidden,
    norm_gain,
    w_query,
    w_key,
    w_value,
    w_out,
    scored_prompt,
    prefix_len,
    state_mask,
):
    xl, z, c = lax.axis_index("xl"), lax.axis_index("z"), lax.axis_index("c")
    xh, y = lax.axis_index("xh"), lax.axis_index("y")
    slots, length, part = state_hidden.shape
    parts = 8
    chips = 16
    piece = length // chips
    rows = slots * length
    length_p = prefix_hidden.shape[1]
    half = w_key.shape[0] // 2
    gain = norm_gain.reshape(parts, 1, part)

    prefix = prefix_hidden[0]
    left, right = turn(prefix, 1), turn(prefix, 3)
    middle = length_p // 2
    across = [turn(left[:middle], 1), turn(right[middle:], 3)]
    blocks = [prefix, left, *across, right]
    w_send = [lax.dynamic_slice_in_dim(w, (1 - xh) * half, half) for w in (w_key, w_value)]
    w_a = swap(jnp.where(c == 0, *w_send), "xh")
    w_b = swap(w_a, "c")

    lane = lax.broadcasted_iota(jnp.int32, (slots, length, HEAD_DIM), 2)
    meta = jnp.where(lane == 0, scored_prompt[0][:, None, None], state_mask[:, :, None])
    meta = jnp.where(lane < 2, meta, 0).astype(BF16)
    packed = jnp.concatenate([state_hidden, meta], axis=2)
    packed = packed.reshape(slots, chips, piece, part + HEAD_DIM).transpose(1, 0, 2, 3)
    here = spread(packed, CHIPS)
    there = swap(here, "c")
    ids = here[:, :, 0, part].astype(jnp.int32)
    ids_there = there[:, :, 0, part].astype(jnp.int32)
    chip = jnp.arange(chips, dtype=jnp.int32)
    wanted = (2 * chip + c)[:, None, None]
    inward = jnp.sum(
        jnp.where(ids[None] == wanted, chip[None, :, None], 0)
        + jnp.where(ids_there[None] == wanted, chips + chip[None, :, None], 0),
        axis=1,
    ).astype(jnp.int32)
    outward = jnp.where(ids % 2 == c, ids // 2, chips + ids // 2)
    routed = spread(select(inward, here, there, [w_a]), CHIPS).reshape(rows, part + HEAD_DIM)

    wide = repeat(routed, parts, part, across)
    wide = spread(wide, TENSOR)
    place = jnp.stack([xh, y, c]).astype(jnp.int32)
    own, back, squares = pl.pallas_call(
        prefix_kernel,
        out_shape=[
            jax.ShapeDtypeStruct((length_p, 2 * HEAD_DIM), F32),
            jax.ShapeDtypeStruct((length_p, 2 * HEAD_DIM), BF16),
            jax.ShapeDtypeStruct((length_p // HEAD_DIM, HEAD_DIM), F32),
        ],
        in_specs=[smem(), vmem()] + [anywhere()] * 9,
        out_specs=[vmem()] * 3,
        scratch_shapes=[
            pltpu.VMEM((4, length_p, part), BF16),
            pltpu.VMEM((half, 4 * HEAD_DIM), BF16),
            pltpu.VMEM((length_p, 4 * HEAD_DIM), F32),
            pltpu.SemaphoreType.DMA((5,)),
            pltpu.SemaphoreType.DMA((4,)),
        ],
        compiler_params=params(18),
        cost_estimate=pl.CostEstimate(flops=2147483648, bytes_accessed=8 << 20, transcendentals=0),
        name="prefix_projection",
    )(place, gain, *blocks, in_hbm(w_key), in_hbm(w_value), w_a, w_b)
    far, far_squares = swap(back, "xh"), swap(squares, "xh")

    q, k, v = pl.pallas_call(
        state_kernel,
        out_shape=[
            jax.ShapeDtypeStruct((rows, w_query.shape[1]), BF16),
            jax.ShapeDtypeStruct((rows, HEAD_DIM), BF16),
            jax.ShapeDtypeStruct((rows, HEAD_DIM), BF16),
        ],
        in_specs=[anywhere(), vmem()] + [anywhere()] * 3,
        out_specs=[vmem()] * 3,
        scratch_shapes=[
            pltpu.VMEM((parts, rows, part), BF16),
            pltpu.VMEM((parts * part, w_query.shape[1] + 2 * HEAD_DIM), BF16),
            pltpu.VMEM((rows, w_query.shape[1] + 2 * HEAD_DIM), F32),
            pltpu.SemaphoreType.DMA((parts,)),
            pltpu.SemaphoreType.DMA((3, parts)),
        ],
        compiler_params=params(14),
        cost_estimate=pl.CostEstimate(flops=1610612736, bytes_accessed=8 << 20, transcendentals=0),
        name="state_projection",
    )(in_hbm(wide), gain, in_hbm(w_query), in_hbm(w_key), in_hbm(w_value))

    limit = lax.dynamic_index_in_dim(prefix_len, (xl * 8 + z) * 2 + c, keepdims=False)
    terms = pl.pallas_call(
        attention_kernel,
        out_shape=jax.ShapeDtypeStruct((parts, rows, part), BF16),
        in_specs=[smem()] + [vmem()] * 9,
        out_specs=vmem(),
        scratch_shapes=[
            pltpu.VMEM((rows, w_out.shape[0]), BF16),
            pltpu.VMEM((length_p, 2 * HEAD_DIM), BF16),
        ],
        compiler_params=params(20),
        cost_estimate=pl.CostEstimate(flops=1800000000, bytes_accessed=8 << 20, transcendentals=1310720),
        name="attention",
    )(limit[None], q, own, far, squares, far_squares, k, v, routed[:, part:], w_out)

    mixed = jnp.sum(spread(terms, TENSOR).astype(F32), axis=0).astype(BF16)
    here = spread(mixed.reshape(chips, slots, piece, part), CHIPS)
    there = swap(here, "c")
    home = spread(select(outward, here, there), CHIPS)
    return home.transpose(1, 0, 2, 3).reshape(slots, length, part)


def solution(mesh):
    split = Mesh(mesh.devices.reshape(2, 8, 2, 2, 4), ("xl", "z", "c", "xh", "y"))
    placed = (
        P(PROMPT, None, TENSOR),
        P(PROMPT, None, TENSOR),
        P(),
        P(None, TENSOR),
        P(None, TENSOR),
        P(None, TENSOR),
        P(TENSOR, None),
        P(PROMPT, None),
        P(),
        P(PROMPT, None),
    )
    return jax.shard_map(
        per_device,
        mesh=split,
        in_specs=placed,
        out_specs=P(PROMPT, None, TENSOR),
        check_vma=False,
    )
```

time: 215 us -> 168 us (0.78)
  waiting for transfers between devices: 74 us -> 37.8 us
  starting transfers between devices: 42.9 us -> 36.5 us
  blocking collectives: 63.3 us -> 59.3 us
  local copies, waits for them, and re-layouts: 11.3 us -> 8.12 us
  Pallas kernels: 18 us -> 21 us
    ppermute x6, waiting for transfers between devices: 36.1 us -> 11.8 us  [swap(): return lax.ppermute(x, axis, [(0, 1), (1, 0)])]
    ppermute x6 -> x4, waiting for transfers between devices: 18.9 us -> 4.31 us  [turn(): return lax.ppermute(x, 'y', [(i, (i + s) % 4) for i in range(4)])]
    ppermute x6 -> x4, starting transfers between devices: 12.7 us -> 6.55 us  [turn(): return lax.ppermute(x, 'y', [(i, (i + s) % 4) for i in range(4)])]
    all_to_all x3, blocking collectives: 63.3 us -> 59.3 us  [spread(): return lax.all_to_all(x, axis, 0, 0, tiled=True)]
    pallas_call x1, Pallas kernels: 3.96 us -> 6.93 us  [per_device(): pl.pallas_call(state_kernel, out_shape=[jax.ShapeDtypeStruct((rows, w_que...]
    all_to_all x3, waiting for transfers between devices: 19 us -> 21.7 us  [spread(): return lax.all_to_all(x, axis, 0, 0, tiled=True)]
    ppermute x6, starting transfers between devices: 9.17 us -> 6.48 us  [swap(): return lax.ppermute(x, axis, [(0, 1), (1, 0)])]
    all_to_all x3, starting transfers between devices: 21 us -> 23.5 us  [spread(): return lax.all_to_all(x, axis, 0, 0, tiled=True)]
  transfers between devices with their start and end apart: 15 -> 13, of which waited for: 9 -> 9; matrix products, arithmetic and copies ran while one was open for 3% -> 2% of each run, Pallas kernels for 5% -> 8%
where the time goes in v2:
time: 168 us
  blocking collectives  59.3 us (35%)
  waiting for transfers between devices  37.8 us (22%)
  starting transfers between devices  36.5 us (22%)
  Pallas kernels  21 us (12%)
  local copies, waits for them, and re-layouts  8.12 us (5%)
  other arithmetic  4.54 us (3%)
    all_to_all x3, blocking collectives, spread(): return lax.all_to_all(x, axis, 0, 0, tiled=True)  59.3 us
    all_to_all x3, starting transfers between devices, spread(): return lax.all_to_all(x, axis, 0, 0, tiled=True)  23.5 us
    all_to_all x3, waiting for transfers between devices, spread(): return lax.all_to_all(x, axis, 0, 0, tiled=True)  21.7 us
    ppermute x6, waiting for transfers between devices, swap(): return lax.ppermute(x, axis, [(0, 1), (1, 0)])  11.8 us
    pallas_call x1, Pallas kernels, per_device(): pl.pallas_call(state_kernel, out_shape=[jax.ShapeDtypeStruct((rows, w_que...  6.93 us
    ppermute x4, starting transfers between devices, turn(): return lax.ppermute(x, 'y', [(i, (i + s) % 4) for i in range(4)])  6.55 us
    ppermute x6, starting transfers between devices, swap(): return lax.ppermute(x, axis, [(0, 1), (1, 0)])  6.48 us
    pallas_call x1, Pallas kernels, per_device(): pl.pallas_call(attention_kernel, out_shape=jax.ShapeDtypeStruct((parts, r...  5.98 us
  transfers between devices with their start and end apart: 13, of which 9 were waited for; matrix products, arithmetic and copies ran while one was open for 2% of the time, Pallas kernels for 8%

profile of v2, /device:TPU:32, one launch (start us, length us, event | category | flops | bytes accessed | tf_op | source)
XLA Modules:
  0.0 167.5 jit_solution(5964582068550340542)
XLA Ops:
  0.8 1.7 %copy_bitcast_fusion = bf16[16,2,8,640]{3,2,1,0:T(8,128)(2,1)} fusion(bf16[2,128,128]{2,1,0:T(8,128)(2,1)S(1)} %select_convert_fusion, bf16[2,128,512]{2,1,0:T(8,128)(2,1)} %param.10), kind=kLoop, calls=%fused_computation.2 | loop fusion | flops 655360 | bytes 655360 | tf_op jit(solution)/shard_map/transpose | solution.py:268
  2.5 9.5 %all-to-all-start = ((bf16[16,2,8,640]{3,2,1,0:T(8,128)(2,1)}), bf16[16,2,8,640]{3,2,1,0:T(8,128)(2,1)S(1)}, u32[]{:S(2)}, u32[]{:S(2)}) async-start(bf16[16,2,8,640]{3,2,1,0:T(8,128)(2,1)} %copy_bitcast_fusion), calls=%async_computation | async-start | bytes 655360 | tf_op jit(solution)/shard_map/all_to_all | solution.py:225
  12.0 1.6 collective-permute-start.2
  13.6 1.7 collective-permute-start.4
  16.6 2.8 %collective-permute-start.1 = (bf16[2048,128]{1,0:T(8,128)(2,1)S(1)}, bf16[2048,128]{1,0:T(8,128)(2,1)S(1)}, u32[]{:S(2)}, u32[]{:S(2)}) collective-permute-start(bf16[2048,128]{1,0:T(8,128)(2,1)S(1)} %dynamic-slice_select_fusion), channel_id=1, source_target_pairs={{0,4},{4,0},{1,5},{5,1},{2,6},{6,2},{3,7},{7,3},{8,12},{12,8},{9,1... | collective-permute-start | bytes 1572872 | tf_op jit(solution)/shard_map/ppermute | solution.py:217
  19.4 3.8 %all-to-all-done.own = bf16[16,2,8,640]{3,2,1,0:T(8,128)(2,1)S(1)} async-done(((bf16[16,2,8,640]{3,2,1,0:T(8,128)(2,1)}), bf16[16,2,8,640]{3,2,1,0:T(8,128)(2,1)S(1)}, u32[]{:S(2)}, u32[]{:S(2)}) %all-to-all-start) | async-done | bytes 327712 | tf_op jit(solution)/shard_map/all_to_all | solution.py:225
  23.3 1.5 collective-permute-done.other
  25.2 7.1 %collective-permute-done.1.rest_0_.refs_7_ = bf16[2048,128]{1,0:T(8,128)(2,1)S(1)} collective-permute-done((bf16[2048,128]{1,0:T(8,128)(2,1)S(1)}, bf16[2048,128]{1,0:T(8,128)(2,1)S(1)}, u32[]{:S(2)}, u32[]{:S(2)}) %collective-permute-start.1) | collective-permute-done | bytes 524320 | tf_op jit(solution)/shard_map/ppermute | solution.py:217
  32.3 1.5 select_blocks.2
  33.8 7.4 %all-to-all-start.1 = ((bf16[16,2,8,640]{3,2,1,0:T(8,128)(2,1)}), bf16[16,2,8,640]{3,2,1,0:T(8,128)(2,1)S(1)}, u32[]{:S(2)}, u32[]{:S(2)}) async-start(bf16[16,2,8,640]{3,2,1,0:T(8,128)(2,1)} %select_blocks.2), calls=%async_computation.1 | async-start | bytes 655360 | tf_op jit(solution)/shard_map/all_to_all | solution.py:225
  44.0 2.7 %collective-permute-start.5 = (bf16[512,512]{1,0:T(8,128)(2,1)S(1)}, bf16[512,512]{1,0:T(8,128)(2,1)S(1)}, u32[]{:S(2)}, u32[]{:S(2)}) collective-permute-start(bf16[512,512]{1,0:T(8,128)(2,1)S(1)} %slice.23), channel_id=1, source_target_pairs={{0,3},{1,0},{2,1},{3,2},{4,7},{5,4},{6,5},{7,6},{8,11},{9,8},{10,9... | collective-permute-start | bytes 1572872 | tf_op jit(solution)/shard_map/ppermute | solution.py:221
  46.7 4.9 %all-to-all-done.1 = bf16[16,2,8,640]{3,2,1,0:T(8,128)(2,1)S(1)} async-done(((bf16[16,2,8,640]{3,2,1,0:T(8,128)(2,1)}), bf16[16,2,8,640]{3,2,1,0:T(8,128)(2,1)S(1)}, u32[]{:S(2)}, u32[]{:S(2)}) %all-to-all-start.1) | async-done | bytes 327712 | tf_op jit(solution)/shard_map/all_to_all | solution.py:225
  51.6 3.9 %collective-permute-done.3.rest_0_.refs_2_ = bf16[512,512]{1,0:T(8,128)(2,1)S(1)} collective-permute-done((bf16[512,512]{1,0:T(8,128)(2,1)S(1)}, bf16[512,512]{1,0:T(8,128)(2,1)S(1)}, u32[]{:S(2)}, u32[]{:S(2)}) %collective-permute-start.3) | collective-permute-done | bytes 524320 | tf_op jit(solution)/shard_map/ppermute | solution.py:221
  55.9 1.4 repeat_rows.1
  57.3 6.5 %all-to-all-start.2 = ((bf16[8,256,512]{2,1,0:T(8,128)(2,1)}), bf16[8,256,512]{2,1,0:T(8,128)(2,1)}, u32[]{:S(2)}, u32[]{:S(2)}) async-start(bf16[8,256,512]{2,1,0:T(8,128)(2,1)} %repeat_rows.1), calls=%async_computation.2 | async-start | bytes 4194304 | tf_op jit(solution)/shard_map/all_to_all | solution.py:225
  64.0 1.8 %collective-permute-done.6.refs_8_ = bf16[2048,128]{1,0:T(8,128)(2,1)S(1)} collective-permute-done((bf16[2048,128]{1,0:T(8,128)(2,1)S(1)}, bf16[2048,128]{1,0:T(8,128)(2,1)S(1)}, u32[]{:S(2)}, u32[]{:S(2)}) %collective-permute-start.6) | collective-permute-done | bytes 524320 | tf_op jit(solution)/shard_map/ppermute | solution.py:217
  70.1 4.5 %prefix_projection.1 = (f32[1024,256]{1,0:T(8,128)S(1)}, bf16[1024,256]{1,0:T(8,128)(2,1)S(1)}, f32[8,128]{1,0:T(8,128)S(1)}) custom-call(s32[3]{0:T(128)S(1)} %pad_add_fusion.where, bf16[8,1,512]{2,1,0:T(2,128)(2,1)S(1)} %reshape.48.gain, bf16[1024,512]{1,0:T(8,128)(2,1)S(1)} %bitcast.23, bf16[1024,512]{1,0:T(8,128)(2,1)S(1)} %copy-done.2, ...), custom_call_target="tpu_custom_call" | custom-call | flops 2147483648 | bytes 8388608 | tf_op jit(solution)/shard_map/prefix_projection/pallas_call | solution.py:286
  74.5 3.6 %collective-permute-start.7 = (bf16[1024,256]{1,0:T(8,128)(2,1)S(1)}, bf16[1024,256]{1,0:T(8,128)(2,1)S(1)}, u32[]{:S(2)}, u32[]{:S(2)}) collective-permute-start(bf16[1024,256]{1,0:T(8,128)(2,1)S(1)} %get-tuple-element.13), channel_id=1, source_target_pairs={{0,4},{4,0},{1,5},{5,1},{2,6},{6,2},{3,7},{7,3},{8,12},{12,8},{9,1... | collective-permute-start | bytes 1572872 | tf_op jit(solution)/shard_map/ppermute | solution.py:217
  78.9 13.0 %all-to-all-done.2.blocks = bf16[8,256,512]{2,1,0:T(8,128)(2,1)} async-done(((bf16[8,256,512]{2,1,0:T(8,128)(2,1)}), bf16[8,256,512]{2,1,0:T(8,128)(2,1)}, u32[]{:S(2)}, u32[]{:S(2)}) %all-to-all-start.2) | async-done | bytes 2097184 | tf_op jit(solution)/shard_map/all_to_all | solution.py:225
  91.8 6.9 %state_projection.1 = (bf16[256,512]{1,0:T(8,128)(2,1)S(1)}, bf16[256,128]{1,0:T(8,128)(2,1)S(1)}, bf16[256,128]{1,0:T(8,128)(2,1)S(1)}) custom-call(bf16[8,256,512]{2,1,0:T(8,128)(2,1)} %all-to-all-done.2.blocks, bf16[8,1,512]{2,1,0:T(2,128)(2,1)S(1)} %reshape.48.gain, bf16[4096,512]{1,0:T(8,128)(2,1)} %w_q.1, bf16[4096,128]{1,0:T(8,128)(2,1)} %refs_5_.1, ...), custom_call_target="tpu_custom_call" | custom-call | flops 1610612736 | bytes 8388608 | tf_op jit(solution)/shard_map/state_projection/pallas_call | solution.py:308
  98.8 6.0 %attention.1 = bf16[8,256,512]{2,1,0:T(8,128)(2,1)S(1)} custom-call(s32[1]{0:T(128)} %dynamic_slice.10.limit, bf16[256,512]{1,0:T(8,128)(2,1)S(1)} %get-tuple-element.11.q, f32[1024,256]{1,0:T(8,128)S(1)} %get-tuple-element.12.own, bf16[1024,256]{1,0:T(8,128)(2,1)S(1)} %collective-permute-done.7.far, f32[8,128]{1,0:T(8,128)S(1)} %get-tuple-element.14.squares, ...), custom_call_target="tpu_custom_call" | custom-call | flops 1800000000 | bytes 8388608 | tf_op jit(solution)/shard_map/attention/pallas_call | solution.py:330
  104.8 28.5 %all_to_all.30 = bf16[8,256,512]{2,1,0:T(8,128)(2,1)S(1)} all-to-all(bf16[8,256,512]{2,1,0:T(8,128)(2,1)S(1)} %attention.1), channel_id=1, replica_groups=mesh['xl'=2,'z'=8,'c'=2,'xh'=2,'y'=4] {'xh','y'}, dimensions={0} | all-to-all | bytes 4194304 | tf_op jit(solution)/shard_map/all_to_all | solution.py:225
  133.6 16.5 %all_to_all.31.own = bf16[16,2,8,512]{3,2,1,0:T(8,128)(2,1)S(1)} all-to-all(bf16[16,2,8,512]{3,2,1,0:T(8,128)(2,1)S(1)} %bitcast.24), channel_id=1, replica_groups=mesh['xl'=2,'z'=8,'c'=2,'xh'=2,'y'=4] {'xl','z'}, dimensions={0} | all-to-all | bytes 524288 | tf_op jit(solution)/shard_map/all_to_all | solution.py:225
  152.4 14.4 %all_to_all.32 = bf16[16,2,8,512]{3,2,1,0:T(8,128)(2,1)S(1)} all-to-all(bf16[16,2,8,512]{3,2,1,0:T(8,128)(2,1)S(1)} %select_blocks.3), channel_id=1, replica_groups=mesh['xl'=2,'z'=8,'c'=2,'xh'=2,'y'=4] {'xl','z'}, dimensions={0} | all-to-all | bytes 524288 | tf_op jit(solution)/shard_map/all_to_all | solution.py:225
  (49 shorter events, 14.2 us)
Async XLA Ops:
  2.5 20.7 %all-to-all-start = ((bf16[16,2,8,640]{3,2,1,0:T(8,128)(2,1)}), bf16[16,2,8,640]{3,2,1,0:T(8,128)(2,1)S(1)}, u32[]{:S(2)}, u32[]{:S(2)}) async-start(bf16[16,2,8,640]{3,2,1,0:T(8,128)(2,1)} %copy_bitcast_fusion), calls=%async_computation | async-start | bytes 655360 | tf_op jit(solution)/shard_map/all_to_all | solution.py:225
  12.0 29.2 %collective-permute-start.2 = (bf16[1024,512]{1,0:T(8,128)(2,1)}, bf16[1024,512]{1,0:T(8,128)(2,1)S(1)}, u32[]{:S(2)}, u32[]{:S(2)}) collective-permute-start(bf16[1024,512]{1,0:T(8,128)(2,1)} %bitcast.21), channel_id=1, source_target_pairs={{0,1},{1,2},{2,3},{3,0},{4,5},{5,6},{6,7},{7,4},{8,9},{9,10},{10,1... | collective-permute-start | bytes 3145736 | tf_op jit(solution)/shard_map/ppermute | solution.py:221
  13.6 29.3 %collective-permute-start.4 = (bf16[1024,512]{1,0:T(8,128)(2,1)}, bf16[1024,512]{1,0:T(8,128)(2,1)}, u32[]{:S(2)}, u32[]{:S(2)}) collective-permute-start(bf16[1024,512]{1,0:T(8,128)(2,1)} %bitcast.22), channel_id=1, source_target_pairs={{0,3},{1,0},{2,1},{3,2},{4,7},{5,4},{6,5},{7,6},{8,11},{9,8},{10,9... | collective-permute-start | bytes 3145736 | tf_op jit(solution)/shard_map/ppermute | solution.py:221
  16.6 15.7 %collective-permute-start.1 = (bf16[2048,128]{1,0:T(8,128)(2,1)S(1)}, bf16[2048,128]{1,0:T(8,128)(2,1)S(1)}, u32[]{:S(2)}, u32[]{:S(2)}) collective-permute-start(bf16[2048,128]{1,0:T(8,128)(2,1)S(1)} %dynamic-slice_select_fusion), channel_id=1, source_target_pairs={{0,4},{4,0},{1,5},{5,1},{2,6},{6,2},{3,7},{7,3},{8,12},{12,8},{9,1... | collective-permute-start | bytes 1572872 | tf_op jit(solution)/shard_map/ppermute | solution.py:217
  23.2 1.6 collective-permute-start
  33.8 17.8 %all-to-all-start.1 = ((bf16[16,2,8,640]{3,2,1,0:T(8,128)(2,1)}), bf16[16,2,8,640]{3,2,1,0:T(8,128)(2,1)S(1)}, u32[]{:S(2)}, u32[]{:S(2)}) async-start(bf16[16,2,8,640]{3,2,1,0:T(8,128)(2,1)} %select_blocks.2), calls=%async_computation.1 | async-start | bytes 655360 | tf_op jit(solution)/shard_map/all_to_all | solution.py:225
  41.3 1.0 copy-start.1
  42.3 13.2 %collective-permute-start.3 = (bf16[512,512]{1,0:T(8,128)(2,1)S(1)}, bf16[512,512]{1,0:T(8,128)(2,1)S(1)}, u32[]{:S(2)}, u32[]{:S(2)}) collective-permute-start(bf16[512,512]{1,0:T(8,128)(2,1)S(1)} %slice.22), channel_id=1, source_target_pairs={{0,1},{1,2},{2,3},{3,0},{4,5},{5,6},{6,7},{7,4},{8,9},{9,10},{10,1... | collective-permute-start | bytes 1572872 | tf_op jit(solution)/shard_map/ppermute | solution.py:221
  44.0 11.9 %collective-permute-start.5 = (bf16[512,512]{1,0:T(8,128)(2,1)S(1)}, bf16[512,512]{1,0:T(8,128)(2,1)S(1)}, u32[]{:S(2)}, u32[]{:S(2)}) collective-permute-start(bf16[512,512]{1,0:T(8,128)(2,1)S(1)} %slice.23), channel_id=1, source_target_pairs={{0,3},{1,0},{2,1},{3,2},{4,7},{5,4},{6,5},{7,6},{8,11},{9,8},{10,9... | collective-permute-start | bytes 1572872 | tf_op jit(solution)/shard_map/ppermute | solution.py:221
  57.3 6.5 %copy-start.6 = (bf16[4096]{0:T(1024)(128)(2,1)S(1)}, bf16[4096]{0:T(1024)(128)(2,1)}, u32[]{:S(2)}) copy-start(bf16[4096]{0:T(1024)(128)(2,1)} %param.12) | copy-start | bytes 24580
  57.3 34.5 %all-to-all-start.2 = ((bf16[8,256,512]{2,1,0:T(8,128)(2,1)}), bf16[8,256,512]{2,1,0:T(8,128)(2,1)}, u32[]{:S(2)}, u32[]{:S(2)}) async-start(bf16[8,256,512]{2,1,0:T(8,128)(2,1)} %repeat_rows.1), calls=%async_computation.2 | async-start | bytes 4194304 | tf_op jit(solution)/shard_map/all_to_all | solution.py:225
  63.9 1.9 %collective-permute-start.6 = (bf16[2048,128]{1,0:T(8,128)(2,1)S(1)}, bf16[2048,128]{1,0:T(8,128)(2,1)S(1)}, u32[]{:S(2)}, u32[]{:S(2)}) collective-permute-start(bf16[2048,128]{1,0:T(8,128)(2,1)S(1)} %collective-permute-done.1.rest_0_.refs_7_), channel_id=1, source_target_pairs={{0,8},{8,0},{1,9},{9,1},{2,10},{10,2},{3,11},{11,3},{4,12},{12,4},... | collective-permute-start | bytes 1572872 | tf_op jit(solution)/shard_map/ppermute | solution.py:217
  65.8 0.8 copy-start.4
  66.6 1.2 copy-start.2
  67.8 1.2 copy-start.3
  69.0 1.0 copy-start.5
  70.1 8.1 %copy-start.7 = (s32[32]{0:T(128)S(1)}, s32[32]{0:T(128)}, u32[]{:S(2)}) copy-start(s32[32]{0:T(128)} %param.18) | copy-start | bytes 388
  74.5 24.2 %collective-permute-start.7 = (bf16[1024,256]{1,0:T(8,128)(2,1)S(1)}, bf16[1024,256]{1,0:T(8,128)(2,1)S(1)}, u32[]{:S(2)}, u32[]{:S(2)}) collective-permute-start(bf16[1024,256]{1,0:T(8,128)(2,1)S(1)} %get-tuple-element.13), channel_id=1, source_target_pairs={{0,4},{4,0},{1,5},{5,1},{2,6},{6,2},{3,7},{7,3},{8,12},{12,8},{9,1... | collective-permute-start | bytes 1572872 | tf_op jit(solution)/shard_map/ppermute | solution.py:217
  78.8 20.0 %collective-permute-start.8 = (f32[8,128]{1,0:T(8,128)S(1)}, f32[8,128]{1,0:T(8,128)S(1)}, u32[]{:S(2)}, u32[]{:S(2)}) collective-permute-start(f32[8,128]{1,0:T(8,128)S(1)} %get-tuple-element.14.squares), channel_id=1, source_target_pairs={{0,4},{4,0},{1,5},{5,1},{2,6},{6,2},{3,7},{7,3},{8,12},{12,8},{9,1... | collective-permute-start | bytes 12296 | tf_op jit(solution)/shard_map/ppermute | solution.py:217
  91.8 7.0 %copy-start = (bf16[512,4096]{1,0:T(8,128)(2,1)S(1)}, bf16[512,4096]{1,0:T(8,128)(2,1)}, u32[]{:S(2)}) copy-start(bf16[512,4096]{1,0:T(8,128)(2,1)} %w_out.1) | copy-start | bytes 12582916
  150.2 1.5 collective-permute-start.9

commit v3 on v2

--- a/solution.py
+++ b/solution.py
@@ -60,7 +60,7 @@
 
 
 def prefix_kernel(where, gain, *refs):
-    blocks, weights, (own, back, squares, x, w, acc, x_sem, w_sem) = refs[:5], refs[5:9], refs[9:]
+    blocks, weights, (own, back, squares, x, w, acc, x_sem, w_sem) = refs[:7], refs[7:11], refs[11:]
     xh, y, c = where[0], where[1], where[2]
     parts, rows, part = x.shape
     w_copies = []
@@ -68,14 +68,14 @@
         source = b.at[pl.ds(pl.multiple_of(xh * parts * part, part), parts * part), :] if k < 2 else b
         w_copies.append(pltpu.make_async_copy(source, w.at[:, pl.ds(k * HEAD_DIM, HEAD_DIM)], w_sem.at[k]))
     middle = rows // 2
-    places = [x.at[0], x.at[1], x.at[2, pl.ds(0, middle), :], x.at[2, pl.ds(middle, middle), :], x.at[3]]
+    places = [x.at[0]] + [x.at[k, pl.ds(r * middle, middle), :] for k in (1, 2, 3) for r in (0, 1)]
     x_copies = [pltpu.make_async_copy(b, p, x_sem.at[k]) for k, (b, p) in enumerate(zip(blocks, places))]
     x_copies[0].start()
     for copy in w_copies + x_copies[1:]:
         copy.start()
     total = jnp.zeros((rows, 1), F32)
     for k in range(parts):
-        for copy in ([x_copies[0]], [x_copies[1]], x_copies[2:4], [x_copies[4]])[k]:
+        for copy in x_copies[:1] if k == 0 else x_copies[2 * k - 1 : 2 * k + 1]:
             copy.wait()
         if k == 0:
             for copy in w_copies:
@@ -99,41 +99,39 @@
         squares[r : r + 1, :] = to_row(total[r * HEAD_DIM : (r + 1) * HEAD_DIM], eye)
 
 
-def state_kernel(blocks, gain, w_q, w_k, w_v, q, k, v, x, w, acc, x_sem, w_sem):
+def state_kernel(x, gain, w_q, w_k, w_v, q, k, v, w, sem):
     parts, rows, part = x.shape
     split = w_q.shape[1]
-    x_copies = [pltpu.make_async_copy(blocks.at[f], x.at[f], x_sem.at[f]) for f in range(parts)]
-    w_copies = []
-    for f in range(parts):
-        at = pl.ds(f * part, part)
-        w_copies.append(
+    half = parts * part // 2
+    copies = []
+    for r in range(2):
+        at = pl.ds(r * half, half)
+        places = (pl.ds(0, split), pl.ds(split, HEAD_DIM), pl.ds(split + HEAD_DIM, HEAD_DIM))
+        copies.append(
             [
-                pltpu.make_async_copy(w_q.at[at, :], w.at[at, pl.ds(0, split)], w_sem.at[0, f]),
-                pltpu.make_async_copy(w_k.at[at, :], w.at[at, pl.ds(split, HEAD_DIM)], w_sem.at[1, f]),
-                pltpu.make_async_copy(w_v.at[at, :], w.at[at, pl.ds(split + HEAD_DIM, HEAD_DIM)], w_sem.at[2, f]),
+                pltpu.make_async_copy(b.at[at, :], w.at[at, p], sem.at[r, j])
+                for j, (b, p) in enumerate(zip((w_q, w_k, w_v), places))
             ]
         )
+    for copy in copies[0] + copies[1]:
+        copy.start()
+    squares = jnp.zeros((rows, part), F32)
+    normed = []
     for f in range(parts):
-        x_copies[f].start()
-        for copy in w_copies[f]:
-            copy.start()
-    total = jnp.zeros((rows, 1), F32)
-    for f in range(parts):
-        x_copies[f].wait()
         h = x[f].astype(F32)
-        total += jnp.sum(h * h, axis=1, keepdims=True)
-        n = (h * gain[f].astype(F32)).astype(BF16)
-        for copy in w_copies[f]:
+        squares += h * h
+        normed.append((h * gain[f].astype(F32)).astype(BF16))
+    scale = inverse_rms(jnp.sum(squares, axis=1, keepdims=True), parts * part)
+    total = None
+    for r in range(2):
+        for copy in copies[r]:
             copy.wait()
-        term = dot(n, w[f * part : (f + 1) * part, :])
-        if f == 0:
-            acc[...] = term
-        else:
-            acc[...] += term
-    scale = inverse_rms(total, parts * part)
-    q[...] = (acc[:, :split] * (scale * HEAD_DIM ** (-0.5))).astype(BF16)
-    k[...] = (acc[:, split : split + HEAD_DIM] * scale).astype(BF16)
-    v[...] = (acc[:, split + HEAD_DIM :] * scale).astype(BF16)
+        n = jnp.concatenate(normed[r * parts // 2 : (r + 1) * parts // 2], axis=1)
+        term = dot(n, w[r * half : (r + 1) * half, :])
+        total = term if r == 0 else total + term
+    q[...] = (total[:, :split] * (scale * HEAD_DIM ** (-0.5))).astype(BF16)
+    k[...] = (total[:, split : split + HEAD_DIM] * scale).astype(BF16)
+    v[...] = (total[:, split + HEAD_DIM :] * scale).astype(BF16)
 
 
 def attention_kernel(limit, q, own, far, squares, far_squares, k, v, meta, w_out, out, att, kv):
@@ -144,7 +142,9 @@
         at = slice(r * HEAD_DIM, (r + 1) * HEAD_DIM)
         total = to_column(squares[r : r + 1, :] + far_squares[r : r + 1, :], eye)
         kv[at, :] = ((own[at, :] + far[at, :].astype(F32)) * inverse_rms(total, 4096)).astype(BF16)
-    near_ok = lax.broadcasted_iota(jnp.int32, (1, length), 1) < limit[0]
+    kv[length:, :HEAD_DIM] = k[...]
+    kv[length:, HEAD_DIM:] = v[...]
+    near = jnp.where(lax.broadcasted_iota(jnp.int32, (1, length), 1) < limit[0], 0.0, -1e30)
     pick = (lax.broadcasted_iota(jnp.int32, (8, HEAD_DIM), 1) == 1).astype(BF16)
     present = dot_t(pick, meta[...])[0:1, :] > 0.5
     a = lax.broadcasted_iota(jnp.int32, (rows, rows), 0)
@@ -154,23 +154,47 @@
     own_ok = same & before & present
     for h in range(q.shape[1] // HEAD_DIM):
         at = slice(h * HEAD_DIM, (h + 1) * HEAD_DIM)
-        qh = q[:, at]
-        s0 = jnp.where(near_ok, dot_t(qh, kv[:, :HEAD_DIM]), -1e30)
-        s1 = jnp.where(own_ok, dot_t(qh, k[...]), -1e30)
+        s = dot_t(q[:, at], kv[:, :HEAD_DIM])
+        s0 = s[:, :length] + near
+        s1 = jnp.where(own_ok, s[:, length:], -1e30)
         top = jnp.maximum(jnp.max(s0, axis=1, keepdims=True), jnp.max(s1, axis=1, keepdims=True))
-        p0 = jnp.where(near_ok, jnp.exp(s0 - top), 0.0)
-        p1 = jnp.where(own_ok, jnp.exp(s1 - top), 0.0)
+        p0 = jnp.exp(s0 - top)
+        p1 = jnp.exp(s1 - top)
         denom = jnp.sum(p0, axis=1, keepdims=True) + jnp.sum(p1, axis=1, keepdims=True)
-        numer = dot(p0.astype(BF16), kv[:, HEAD_DIM:]) + dot(p1.astype(BF16), v[...])
+        p = jnp.concatenate([p0.astype(BF16), p1.astype(BF16)], axis=1)
+        numer = dot(p, kv[:, HEAD_DIM:])
         att[:, at] = (numer / denom).astype(BF16)
     part = out.shape[2]
-
-    def project(t, carry):
-        at = pl.ds(pl.multiple_of(t * part, part), part)
-        out[t] = dot(att[...], w_out[:, at]).astype(BF16)
-        return carry
-
-    lax.fori_loop(0, out.shape[0], project, 0)
+    for t in range(out.shape[0]):
+        out[t] = dot(att[...], w_out[:, t * part : (t + 1) * part]).astype(BF16)
+
+
+def pack_kernel(where, ids, hidden, mask, prefix, w_k, w_v, out, top, bottom, w_half, sem):
+    slots, length, part = hidden.shape
+    pieces = length // 8
+    middle = prefix.shape[0] // 2
+    half = w_half.shape[0]
+    rows = pl.ds(pl.multiple_of((1 - where[0]) * half, half), half)
+    halves = [
+        pltpu.make_async_copy(prefix.at[pl.ds(0, middle), :], top, sem.at[0]),
+        pltpu.make_async_copy(prefix.at[pl.ds(middle, middle), :], bottom, sem.at[1]),
+    ]
+    key = pltpu.make_async_copy(w_k.at[rows, :], w_half, sem.at[2])
+    value = pltpu.make_async_copy(w_v.at[rows, :], w_half, sem.at[2])
+    for copy in halves:
+        copy.start()
+    pl.when(where[2] == 0)(key.start)
+    pl.when(where[2] != 0)(value.start)
+    eye = unit(length)
+    lane = lax.broadcasted_iota(jnp.int32, (length, HEAD_DIM), 1)
+    for s in range(slots):
+        present = to_column(mask[s : s + 1, :].astype(F32), eye)
+        meta = jnp.where(lane == 0, ids[0, s].astype(F32), jnp.where(lane == 1, present, 0.0))
+        out[:, s, :, :part] = hidden[s].astype(F32).reshape(pieces, 8, part).astype(BF16)
+        out[:, s, :, part:] = meta.reshape(pieces, 8, HEAD_DIM).astype(BF16)
+    for copy in halves:
+        copy.wait()
+    key.wait()
 
 
 def select_kernel(index, own, other, *rest):
@@ -199,6 +223,22 @@
         cost_estimate=pl.CostEstimate(flops=0, bytes_accessed=2 << 20, transcendentals=0),
         name="repeat_rows",
     )(x, *after)
+
+
+def mark_kernel(*refs):
+    refs[-1][...] = jnp.zeros(refs[-1].shape, F32)
+
+
+def mark(after, flops):
+    return pl.pallas_call(
+        mark_kernel,
+        out_shape=jax.ShapeDtypeStruct((8, HEAD_DIM), F32),
+        in_specs=[anywhere()] * len(after),
+        out_specs=vmem(),
+        compiler_params=params(2),
+        cost_estimate=pl.CostEstimate(flops=flops, bytes_accessed=4096, transcendentals=0),
+        name="arrived",
+    )(*after)
 
 
 def select(index, own, other, after=()):
@@ -252,20 +292,31 @@
     half = w_key.shape[0] // 2
     gain = norm_gain.reshape(parts, 1, part)
 
+    place = jnp.stack([xh, y, c]).astype(jnp.int32)
     prefix = prefix_hidden[0]
-    left, right = turn(prefix, 1), turn(prefix, 3)
     middle = length_p // 2
-    across = [turn(left[:middle], 1), turn(right[middle:], 3)]
-    blocks = [prefix, left, *across, right]
-    w_send = [lax.dynamic_slice_in_dim(w, (1 - xh) * half, half) for w in (w_key, w_value)]
-    w_a = swap(jnp.where(c == 0, *w_send), "xh")
+    packed, top, bottom, w_send = pl.pallas_call(
+        pack_kernel,
+        out_shape=[
+            jax.ShapeDtypeStruct((chips, slots, piece, part + HEAD_DIM), BF16),
+            jax.ShapeDtypeStruct((middle, part), BF16),
+            jax.ShapeDtypeStruct((middle, part), BF16),
+            jax.ShapeDtypeStruct((half, HEAD_DIM), BF16),
+        ],
+        in_specs=[smem(), smem(), vmem(), vmem()] + [anywhere()] * 3,
+        out_specs=[vmem()] * 4,
+        scratch_shapes=[pltpu.SemaphoreType.DMA((3,))],
+        compiler_params=params(10),
+        cost_estimate=pl.CostEstimate(flops=0, bytes_accessed=4 << 20, transcendentals=0),
+        name="pack_states",
+    )(place, in_hbm(scored_prompt), *[in_hbm(x) for x in (state_hidden, state_mask, prefix, w_key, w_value)])
+
+    first = [turn(top, 1), turn(bottom, 3)]
+    second = [turn(bottom, 1), turn(top, 3), turn(first[0], 1), turn(first[1], 3)]
+    blocks = [prefix, first[0], second[0], second[2], second[3], second[1], first[1]]
+    w_a = swap(w_send, "xh")
     w_b = swap(w_a, "c")
 
-    lane = lax.broadcasted_iota(jnp.int32, (slots, length, HEAD_DIM), 2)
-    meta = jnp.where(lane == 0, scored_prompt[0][:, None, None], state_mask[:, :, None])
-    meta = jnp.where(lane < 2, meta, 0).astype(BF16)
-    packed = jnp.concatenate([state_hidden, meta], axis=2)
-    packed = packed.reshape(slots, chips, piece, part + HEAD_DIM).transpose(1, 0, 2, 3)
     here = spread(packed, CHIPS)
     there = swap(here, "c")
     ids = here[:, :, 0, part].astype(jnp.int32)
@@ -278,11 +329,10 @@
         axis=1,
     ).astype(jnp.int32)
     outward = jnp.where(ids % 2 == c, ids // 2, chips + ids // 2)
-    routed = spread(select(inward, here, there, [w_a]), CHIPS).reshape(rows, part + HEAD_DIM)
-
-    wide = repeat(routed, parts, part, across)
+    routed = spread(select(inward, here, there, [mark(first, 10**9)]), CHIPS).reshape(rows, part + HEAD_DIM)
+
+    wide = repeat(routed, parts, part, [mark(second, 10**9), w_b])
     wide = spread(wide, TENSOR)
-    place = jnp.stack([xh, y, c]).astype(jnp.int32)
     own, back, squares = pl.pallas_call(
         prefix_kernel,
         out_shape=[
@@ -290,19 +340,19 @@
             jax.ShapeDtypeStruct((length_p, 2 * HEAD_DIM), BF16),
             jax.ShapeDtypeStruct((length_p // HEAD_DIM, HEAD_DIM), F32),
         ],
-        in_specs=[smem(), vmem()] + [anywhere()] * 9,
+        in_specs=[smem(), vmem()] + [anywhere()] * 11,
         out_specs=[vmem()] * 3,
         scratch_shapes=[
             pltpu.VMEM((4, length_p, part), BF16),
             pltpu.VMEM((half, 4 * HEAD_DIM), BF16),
             pltpu.VMEM((length_p, 4 * HEAD_DIM), F32),
-            pltpu.SemaphoreType.DMA((5,)),
+            pltpu.SemaphoreType.DMA((7,)),
             pltpu.SemaphoreType.DMA((4,)),
         ],
         compiler_params=params(18),
         cost_estimate=pl.CostEstimate(flops=2147483648, bytes_accessed=8 << 20, transcendentals=0),
         name="prefix_projection",
-    )(place, gain, *blocks, in_hbm(w_key), in_hbm(w_value), w_a, w_b)
+    )(place, gain, *[in_hbm(x) for x in [*blocks, w_key, w_value, w_a, w_b]])
     far, far_squares = swap(back, "xh"), swap(squares, "xh")
 
     q, k, v = pl.pallas_call(
@@ -312,19 +362,16 @@
             jax.ShapeDtypeStruct((rows, HEAD_DIM), BF16),
             jax.ShapeDtypeStruct((rows, HEAD_DIM), BF16),
         ],
-        in_specs=[anywhere(), vmem()] + [anywhere()] * 3,
+        in_specs=[vmem()] * 2 + [anywhere()] * 3,
         out_specs=[vmem()] * 3,
         scratch_shapes=[
-            pltpu.VMEM((parts, rows, part), BF16),
             pltpu.VMEM((parts * part, w_query.shape[1] + 2 * HEAD_DIM), BF16),
-            pltpu.VMEM((rows, w_query.shape[1] + 2 * HEAD_DIM), F32),
-            pltpu.SemaphoreType.DMA((parts,)),
-            pltpu.SemaphoreType.DMA((3, parts)),
-        ],
-        compiler_params=params(14),
+            pltpu.SemaphoreType.DMA((2, 3)),
+        ],
+        compiler_params=params(20),
         cost_estimate=pl.CostEstimate(flops=1610612736, bytes_accessed=8 << 20, transcendentals=0),
         name="state_projection",
-    )(in_hbm(wide), gain, in_hbm(w_query), in_hbm(w_key), in_hbm(w_value))
+    )(wide, gain, in_hbm(w_query), in_hbm(w_key), in_hbm(w_value))
 
     limit = lax.dynamic_index_in_dim(prefix_len, (xl * 8 + z) * 2 + c, keepdims=False)
     terms = pl.pallas_call(
@@ -334,9 +381,9 @@
         out_specs=vmem(),
         scratch_shapes=[
             pltpu.VMEM((rows, w_out.shape[0]), BF16),
-            pltpu.VMEM((length_p, 2 * HEAD_DIM), BF16),
-        ],
-        compiler_params=params(20),
+            pltpu.VMEM((length_p + rows, 2 * HEAD_DIM), BF16),
+        ],
+        compiler_params=params(24),
         cost_estimate=pl.CostEstimate(flops=1800000000, bytes_accessed=8 << 20, transcendentals=1310720),
         name="attention",
     )(limit[None], q, own, far, squares, far_squares, k, v, routed[:, part:], w_out)

time: 168 us -> 165 us (0.982)
  local copies, waits for them, and re-layouts: 8.12 us -> 1.72 us
  Pallas kernels: 21 us -> 25 us
  other arithmetic: 4.54 us -> 0.69 us
    ppermute x6, waiting for transfers between devices: 11.8 us -> 3.08 us  [swap(): return lax.ppermute(x, axis, [(0, 1), (1, 0)])]
    ppermute x4 -> x6, waiting for transfers between devices: 4.31 us -> 10.3 us  [turn(): return lax.ppermute(x, 'y', [(i, (i + s) % 4) for i in range(4)])]
    unnamed x16 -> x20, local copies, waits for them, and re-layouts: 5.27 us -> 0.04 us
    all_to_all x3, waiting for transfers between devices: 21.7 us -> 25.7 us  [spread(): return lax.all_to_all(x, axis, 0, 0, tiled=True)]
    pallas_call x0 -> x3, Pallas kernels: none -> 3.65 us  [the longest x1 3.65 us: per_device(): pl.pallas_call(pack_kernel, out_shape=[jax.ShapeDtypeStruct((chips, slots...]
    ppermute x4 -> x6, starting transfers between devices: 6.55 us -> 9.77 us  [turn(): return lax.ppermute(x, 'y', [(i, (i + s) % 4) for i in range(4)])]
    all_to_all x3, starting transfers between devices: 23.5 us -> 20.7 us  [spread(): return lax.all_to_all(x, axis, 0, 0, tiled=True)]
    pallas_call x1, Pallas kernels: 4.46 us -> 6.62 us  [per_device(): pl.pallas_call(prefix_kernel, out_shape=[jax.ShapeDtypeStruct((length_p,...]
  transfers between devices with their start and end apart: 13 -> 15, of which waited for: 9 -> 7; matrix products, arithmetic and copies ran while one was open for 2% -> 1% of each run, Pallas kernels for 8% -> 8%
where the time goes in v3:
time: 165 us; the launch traced here: 164 us
  blocking collectives  60.5 us (37%)
  waiting for transfers between devices  39.1 us (24%)
  starting transfers between devices  36.9 us (22%)
  Pallas kernels  25 us (15%)
  local copies, waits for them, and re-layouts  1.72 us (1%)
    all_to_all x3, blocking collectives, spread(): return lax.all_to_all(x, axis, 0, 0, tiled=True)  60.5 us
    all_to_all x3, waiting for transfers between devices, spread(): return lax.all_to_all(x, axis, 0, 0, tiled=True)  25.7 us
    all_to_all x3, starting transfers between devices, spread(): return lax.all_to_all(x, axis, 0, 0, tiled=True)  20.7 us
    ppermute x6, waiting for transfers between devices, turn(): return lax.ppermute(x, 'y', [(i, (i + s) % 4) for i in range(4)])  10.3 us
    ppermute x6, starting transfers between devices, turn(): return lax.ppermute(x, 'y', [(i, (i + s) % 4) for i in range(4)])  9.77 us
    pallas_call x1, Pallas kernels, per_device(): pl.pallas_call(prefix_kernel, out_shape=[jax.ShapeDtypeStruct((length_p,...  6.62 us
    ppermute x6, starting transfers between devices, swap(): return lax.ppermute(x, axis, [(0, 1), (1, 0)])  6.44 us
    pallas_call x1, Pallas kernels, per_device(): pl.pallas_call(state_kernel, out_shape=[jax.ShapeDtypeStruct((rows, w_que...  5.5 us
  transfers between devices with their start and end apart: 15, of which 7 were waited for; matrix products, arithmetic and copies ran while one was open for 1% of the time, Pallas kernels for 8%

profile of v3, /device:TPU:32, one launch (start us, length us, event | category | flops | bytes accessed | tf_op | source)
XLA Modules:
  0.0 164.0 jit_solution(6803246047028838446)
XLA Ops:
  0.1 3.6 %pack_states.1 = (bf16[16,2,8,640]{3,2,1,0:T(8,128)(2,1)}, bf16[512,512]{1,0:T(8,128)(2,1)}, bf16[512,512]{1,0:T(8,128)(2,1)}, bf16[2048,128]{1,0:T(8,128)(2,1)}) custom-call(s32[3]{0:T(128)S(1)} %pad_add_fusion.where, s32[1,2]{1,0:T(1,128)} %ids.1, bf16[2,128,512]{2,1,0:T(8,128)(2,1)} %hidden.1, s32[2,128]{1,0:T(2,128)} %mask.1, ...), custom_call_target="tpu_custom_call" | custom-call | bytes 4194304 | tf_op jit(solution)/shard_map/pack_states/pallas_call | solution.py:298
  3.7 9.5 %all-to-all-start = ((bf16[16,2,8,640]{3,2,1,0:T(8,128)(2,1)}), bf16[16,2,8,640]{3,2,1,0:T(8,128)(2,1)S(1)}, u32[]{:S(2)}, u32[]{:S(2)}) async-start(bf16[16,2,8,640]{3,2,1,0:T(8,128)(2,1)} %get-tuple-element.15), calls=%async_computation | async-start | bytes 655360 | tf_op jit(solution)/shard_map/all_to_all | solution.py:265
  13.3 1.6 collective-permute-start.1
  14.8 1.7 %collective-permute-start.2 = (bf16[512,512]{1,0:T(8,128)(2,1)}, bf16[512,512]{1,0:T(8,128)(2,1)S(1)}, u32[]{:S(2)}, u32[]{:S(2)}) collective-permute-start(bf16[512,512]{1,0:T(8,128)(2,1)} %get-tuple-element.17), channel_id=1, source_target_pairs={{0,3},{1,0},{2,1},{3,2},{4,7},{5,4},{6,5},{7,6},{8,11},{9,8},{10,9... | collective-permute-start | bytes 1572872 | tf_op jit(solution)/shard_map/ppermute | solution.py:261
  16.9 2.9 %collective-permute-start.4 = (bf16[512,512]{1,0:T(8,128)(2,1)}, bf16[512,512]{1,0:T(8,128)(2,1)S(1)}, u32[]{:S(2)}, u32[]{:S(2)}) collective-permute-start(bf16[512,512]{1,0:T(8,128)(2,1)} %get-tuple-element.16), channel_id=1, source_target_pairs={{0,3},{1,0},{2,1},{3,2},{4,7},{5,4},{6,5},{7,6},{8,11},{9,8},{10,9... | collective-permute-start | bytes 1572872 | tf_op jit(solution)/shard_map/ppermute | solution.py:261
  19.7 4.7 %all-to-all-done.own = bf16[16,2,8,640]{3,2,1,0:T(8,128)(2,1)S(1)} async-done(((bf16[16,2,8,640]{3,2,1,0:T(8,128)(2,1)}), bf16[16,2,8,640]{3,2,1,0:T(8,128)(2,1)S(1)}, u32[]{:S(2)}, u32[]{:S(2)}) %all-to-all-start) | async-done | bytes 327712 | tf_op jit(solution)/shard_map/all_to_all | solution.py:265
  24.5 5.1 %collective-permute-done.1.refs_0_.refs_1_ = bf16[512,512]{1,0:T(8,128)(2,1)S(1)} collective-permute-done((bf16[512,512]{1,0:T(8,128)(2,1)}, bf16[512,512]{1,0:T(8,128)(2,1)S(1)}, u32[]{:S(2)}, u32[]{:S(2)}) %collective-permute-start.1) | collective-permute-done | bytes 524320 | tf_op jit(solution)/shard_map/ppermute | solution.py:261
  29.5 2.7 %collective-permute-start.7 = (bf16[2048,128]{1,0:T(8,128)(2,1)}, bf16[2048,128]{1,0:T(8,128)(2,1)}, u32[]{:S(2)}, u32[]{:S(2)}) collective-permute-start(bf16[2048,128]{1,0:T(8,128)(2,1)} %get-tuple-element.18), channel_id=1, source_target_pairs={{0,4},{4,0},{1,5},{5,1},{2,6},{6,2},{3,7},{7,3},{8,12},{12,8},{9,1... | collective-permute-start | bytes 1572872 | tf_op jit(solution)/shard_map/ppermute | solution.py:257
  32.8 2.9 %collective-permute-start.6 = (bf16[512,512]{1,0:T(8,128)(2,1)S(1)}, bf16[512,512]{1,0:T(8,128)(2,1)}, u32[]{:S(2)}, u32[]{:S(2)}) collective-permute-start(bf16[512,512]{1,0:T(8,128)(2,1)S(1)} %collective-permute-done.2.refs_1_.refs_6_), channel_id=1, source_target_pairs={{0,3},{1,0},{2,1},{3,2},{4,7},{5,4},{6,5},{7,6},{8,11},{9,8},{10,9... | collective-permute-start | bytes 1572872 | tf_op jit(solution)/shard_map/ppermute | solution.py:261
  36.1 1.5 select_blocks.2
  37.6 7.5 %all-to-all-start.1 = ((bf16[16,2,8,640]{3,2,1,0:T(8,128)(2,1)}), bf16[16,2,8,640]{3,2,1,0:T(8,128)(2,1)S(1)}, u32[]{:S(2)}, u32[]{:S(2)}) async-start(bf16[16,2,8,640]{3,2,1,0:T(8,128)(2,1)} %select_blocks.2), calls=%async_computation.1 | async-start | bytes 655360 | tf_op jit(solution)/shard_map/all_to_all | solution.py:265
  45.2 5.2 %collective-permute-done.5.refs_2_.refs_3_ = bf16[512,512]{1,0:T(8,128)(2,1)} collective-permute-done((bf16[512,512]{1,0:T(8,128)(2,1)S(1)}, bf16[512,512]{1,0:T(8,128)(2,1)}, u32[]{:S(2)}, u32[]{:S(2)}) %collective-permute-start.5) | collective-permute-done | bytes 524320 | tf_op jit(solution)/shard_map/ppermute | solution.py:261
  50.5 4.1 %all-to-all-done.1 = bf16[16,2,8,640]{3,2,1,0:T(8,128)(2,1)S(1)} async-done(((bf16[16,2,8,640]{3,2,1,0:T(8,128)(2,1)}), bf16[16,2,8,640]{3,2,1,0:T(8,128)(2,1)S(1)}, u32[]{:S(2)}, u32[]{:S(2)}) %all-to-all-start.1) | async-done | bytes 327712 | tf_op jit(solution)/shard_map/all_to_all | solution.py:265
  54.6 1.5 repeat_rows.1
  56.1 3.6 %all-to-all-start.2 = ((bf16[8,256,512]{2,1,0:T(8,128)(2,1)}), bf16[8,256,512]{2,1,0:T(8,128)(2,1)S(1)}, u32[]{:S(2)}, u32[]{:S(2)}) async-start(bf16[8,256,512]{2,1,0:T(8,128)(2,1)} %repeat_rows.1), calls=%async_computation.2 | async-start | bytes 4194304 | tf_op jit(solution)/shard_map/all_to_all | solution.py:265
  59.7 6.6 %prefix_projection.1 = (f32[1024,256]{1,0:T(8,128)S(1)}, bf16[1024,256]{1,0:T(8,128)(2,1)}, f32[8,128]{1,0:T(8,128)}) custom-call(s32[3]{0:T(128)S(1)} %pad_add_fusion.where, bf16[8,1,512]{2,1,0:T(2,128)(2,1)S(1)} %reshape.42.gain, bf16[1024,512]{1,0:T(8,128)(2,1)} %bitcast.16, bf16[512,512]{1,0:T(8,128)(2,1)} %copy-done.2, bf16[512,512]{1,0:T(8,128)(2,1)} %copy-done.4, ...), custom_call_target="tpu_custom_call" | custom-call | flops 2147483648 | bytes 8388608 | tf_op jit(solution)/shard_map/prefix_projection/pallas_call | solution.py:336
  66.3 3.5 %collective-permute-start.9 = (bf16[1024,256]{1,0:T(8,128)(2,1)}, bf16[1024,256]{1,0:T(8,128)(2,1)}, u32[]{:S(2)}, u32[]{:S(2)}) collective-permute-start(bf16[1024,256]{1,0:T(8,128)(2,1)} %get-tuple-element.21), channel_id=1, source_target_pairs={{0,4},{4,0},{1,5},{5,1},{2,6},{6,2},{3,7},{7,3},{8,12},{12,8},{9,1... | collective-permute-start | bytes 1572872 | tf_op jit(solution)/shard_map/ppermute | solution.py:257
  70.6 16.9 %all-to-all-done.2.x = bf16[8,256,512]{2,1,0:T(8,128)(2,1)S(1)} async-done(((bf16[8,256,512]{2,1,0:T(8,128)(2,1)}), bf16[8,256,512]{2,1,0:T(8,128)(2,1)S(1)}, u32[]{:S(2)}, u32[]{:S(2)}) %all-to-all-start.2) | async-done | bytes 2097184 | tf_op jit(solution)/shard_map/all_to_all | solution.py:265
  87.4 5.5 %state_projection.1 = (bf16[256,512]{1,0:T(8,128)(2,1)S(1)}, bf16[256,128]{1,0:T(8,128)(2,1)S(1)}, bf16[256,128]{1,0:T(8,128)(2,1)S(1)}) custom-call(bf16[8,256,512]{2,1,0:T(8,128)(2,1)S(1)} %all-to-all-done.2.x, bf16[8,1,512]{2,1,0:T(2,128)(2,1)S(1)} %reshape.42.gain, bf16[4096,512]{1,0:T(8,128)(2,1)} %w_q.1, bf16[4096,128]{1,0:T(8,128)(2,1)} %refs_7_.1, ...), custom_call_target="tpu_custom_call" | custom-call | flops 1610612736 | bytes 8388608 | tf_op jit(solution)/shard_map/state_projection/pallas_call | solution.py:358
  93.0 1.6 %collective-permute-done.10.far_squares = f32[8,128]{1,0:T(8,128)} collective-permute-done((f32[8,128]{1,0:T(8,128)}, f32[8,128]{1,0:T(8,128)}, u32[]{:S(2)}, u32[]{:S(2)}) %collective-permute-start.10) | collective-permute-done | bytes 4128 | tf_op jit(solution)/shard_map/ppermute | solution.py:257
  94.6 5.5 %attention.1 = bf16[8,256,512]{2,1,0:T(8,128)(2,1)S(1)} custom-call(s32[1]{0:T(128)} %dynamic_slice.4.limit, bf16[256,512]{1,0:T(8,128)(2,1)S(1)} %get-tuple-element.19.q, f32[1024,256]{1,0:T(8,128)S(1)} %get-tuple-element.20.own, bf16[1024,256]{1,0:T(8,128)(2,1)} %collective-permute-done.9.far, f32[8,128]{1,0:T(8,128)} %get-tuple-element.22.squares, ...), custom_call_target="tpu_custom_call" | custom-call | flops 1800000000 | bytes 8388608 | tf_op jit(solution)/shard_map/attention/pallas_call | solution.py:377
  100.1 28.4 %all_to_all.30 = bf16[8,256,512]{2,1,0:T(8,128)(2,1)S(1)} all-to-all(bf16[8,256,512]{2,1,0:T(8,128)(2,1)S(1)} %attention.1), channel_id=1, replica_groups=mesh['xl'=2,'z'=8,'c'=2,'xh'=2,'y'=4] {'xh','y'}, dimensions={0} | all-to-all | bytes 4194304 | tf_op jit(solution)/shard_map/all_to_all | solution.py:265
  128.9 17.7 %all_to_all.31.own = bf16[16,2,8,512]{3,2,1,0:T(8,128)(2,1)S(1)} all-to-all(bf16[16,2,8,512]{3,2,1,0:T(8,128)(2,1)S(1)} %bitcast.17), channel_id=1, replica_groups=mesh['xl'=2,'z'=8,'c'=2,'xh'=2,'y'=4] {'xl','z'}, dimensions={0} | all-to-all | bytes 524288 | tf_op jit(solution)/shard_map/all_to_all | solution.py:265
  148.9 14.4 %all_to_all.32 = bf16[16,2,8,512]{3,2,1,0:T(8,128)(2,1)S(1)} all-to-all(bf16[16,2,8,512]{3,2,1,0:T(8,128)(2,1)S(1)} %select_blocks.3), channel_id=1, replica_groups=mesh['xl'=2,'z'=8,'c'=2,'xh'=2,'y'=4] {'xl','z'}, dimensions={0} | all-to-all | bytes 524288 | tf_op jit(solution)/shard_map/all_to_all | solution.py:265
  (53 shorter events, 5.5 us)
Async XLA Ops:
  3.7 20.7 %all-to-all-start = ((bf16[16,2,8,640]{3,2,1,0:T(8,128)(2,1)}), bf16[16,2,8,640]{3,2,1,0:T(8,128)(2,1)S(1)}, u32[]{:S(2)}, u32[]{:S(2)}) async-start(bf16[16,2,8,640]{3,2,1,0:T(8,128)(2,1)} %get-tuple-element.15), calls=%async_computation | async-start | bytes 655360 | tf_op jit(solution)/shard_map/all_to_all | solution.py:265
  13.3 16.3 %collective-permute-start.1 = (bf16[512,512]{1,0:T(8,128)(2,1)}, bf16[512,512]{1,0:T(8,128)(2,1)S(1)}, u32[]{:S(2)}, u32[]{:S(2)}) collective-permute-start(bf16[512,512]{1,0:T(8,128)(2,1)} %get-tuple-element.16), channel_id=1, source_target_pairs={{0,1},{1,2},{2,3},{3,0},{4,5},{5,6},{6,7},{7,4},{8,9},{9,10},{10,1... | collective-permute-start | bytes 1572872 | tf_op jit(solution)/shard_map/ppermute | solution.py:261
  14.8 17.4 %collective-permute-start.2 = (bf16[512,512]{1,0:T(8,128)(2,1)}, bf16[512,512]{1,0:T(8,128)(2,1)S(1)}, u32[]{:S(2)}, u32[]{:S(2)}) collective-permute-start(bf16[512,512]{1,0:T(8,128)(2,1)} %get-tuple-element.17), channel_id=1, source_target_pairs={{0,3},{1,0},{2,1},{3,2},{4,7},{5,4},{6,5},{7,6},{8,11},{9,8},{10,9... | collective-permute-start | bytes 1572872 | tf_op jit(solution)/shard_map/ppermute | solution.py:261
  16.5 28.7 %collective-permute-start.3 = (bf16[512,512]{1,0:T(8,128)(2,1)}, bf16[512,512]{1,0:T(8,128)(2,1)S(1)}, u32[]{:S(2)}, u32[]{:S(2)}) collective-permute-start(bf16[512,512]{1,0:T(8,128)(2,1)} %get-tuple-element.17), channel_id=1, source_target_pairs={{0,1},{1,2},{2,3},{3,0},{4,5},{5,6},{6,7},{7,4},{8,9},{9,10},{10,1... | collective-permute-start | bytes 1572872 | tf_op jit(solution)/shard_map/ppermute | solution.py:261
  16.9 28.4 %collective-permute-start.4 = (bf16[512,512]{1,0:T(8,128)(2,1)}, bf16[512,512]{1,0:T(8,128)(2,1)S(1)}, u32[]{:S(2)}, u32[]{:S(2)}) collective-permute-start(bf16[512,512]{1,0:T(8,128)(2,1)} %get-tuple-element.16), channel_id=1, source_target_pairs={{0,3},{1,0},{2,1},{3,2},{4,7},{5,4},{6,5},{7,6},{8,11},{9,8},{10,9... | collective-permute-start | bytes 1572872 | tf_op jit(solution)/shard_map/ppermute | solution.py:261
  24.4 8.3 %collective-permute-start = (bf16[16,2,8,640]{3,2,1,0:T(8,128)(2,1)S(1)}, bf16[16,2,8,640]{3,2,1,0:T(8,128)(2,1)S(1)}, u32[]{:S(2)}, u32[]{:S(2)}) collective-permute-start(bf16[16,2,8,640]{3,2,1,0:T(8,128)(2,1)S(1)} %all-to-all-done.own), channel_id=1, source_target_pairs={{0,8},{8,0},{1,9},{9,1},{2,10},{10,2},{3,11},{11,3},{4,12},{12,4},... | collective-permute-start | bytes 983048 | tf_op jit(solution)/shard_map/ppermute | solution.py:257
  29.5 8.0 %copy-start.2 = (bf16[512,512]{1,0:T(8,128)(2,1)}, bf16[512,512]{1,0:T(8,128)(2,1)S(1)}, u32[]{:S(2)}) copy-start(bf16[512,512]{1,0:T(8,128)(2,1)S(1)} %collective-permute-done.1.refs_0_.refs_1_) | copy-start | bytes 1572868
  29.5 15.6 %collective-permute-start.7 = (bf16[2048,128]{1,0:T(8,128)(2,1)}, bf16[2048,128]{1,0:T(8,128)(2,1)}, u32[]{:S(2)}, u32[]{:S(2)}) collective-permute-start(bf16[2048,128]{1,0:T(8,128)(2,1)} %get-tuple-element.18), channel_id=1, source_target_pairs={{0,4},{4,0},{1,5},{5,1},{2,6},{6,2},{3,7},{7,3},{8,12},{12,8},{9,1... | collective-permute-start | bytes 1572872 | tf_op jit(solution)/shard_map/ppermute | solution.py:257
  32.3 5.3 %copy-start.3 = (bf16[512,512]{1,0:T(8,128)(2,1)}, bf16[512,512]{1,0:T(8,128)(2,1)S(1)}, u32[]{:S(2)}) copy-start(bf16[512,512]{1,0:T(8,128)(2,1)S(1)} %collective-permute-done.2.refs_1_.refs_6_) | copy-start | bytes 1572868
  32.3 18.1 %collective-permute-start.5 = (bf16[512,512]{1,0:T(8,128)(2,1)S(1)}, bf16[512,512]{1,0:T(8,128)(2,1)}, u32[]{:S(2)}, u32[]{:S(2)}) collective-permute-start(bf16[512,512]{1,0:T(8,128)(2,1)S(1)} %collective-permute-done.1.refs_0_.refs_1_), channel_id=1, source_target_pairs={{0,1},{1,2},{2,3},{3,0},{4,5},{5,6},{6,7},{7,4},{8,9},{9,10},{10,1... | collective-permute-start | bytes 1572872 | tf_op jit(solution)/shard_map/ppermute | solution.py:261
  32.8 17.7 %collective-permute-start.6 = (bf16[512,512]{1,0:T(8,128)(2,1)S(1)}, bf16[512,512]{1,0:T(8,128)(2,1)}, u32[]{:S(2)}, u32[]{:S(2)}) collective-permute-start(bf16[512,512]{1,0:T(8,128)(2,1)S(1)} %collective-permute-done.2.refs_1_.refs_6_), channel_id=1, source_target_pairs={{0,3},{1,0},{2,1},{3,2},{4,7},{5,4},{6,5},{7,6},{8,11},{9,8},{10,9... | collective-permute-start | bytes 1572872 | tf_op jit(solution)/shard_map/ppermute | solution.py:261
  37.6 17.0 %all-to-all-start.1 = ((bf16[16,2,8,640]{3,2,1,0:T(8,128)(2,1)}), bf16[16,2,8,640]{3,2,1,0:T(8,128)(2,1)S(1)}, u32[]{:S(2)}, u32[]{:S(2)}) async-start(bf16[16,2,8,640]{3,2,1,0:T(8,128)(2,1)} %select_blocks.2), calls=%async_computation.1 | async-start | bytes 655360 | tf_op jit(solution)/shard_map/all_to_all | solution.py:265
  45.1 5.3 %collective-permute-start.8 = (bf16[2048,128]{1,0:T(8,128)(2,1)}, bf16[2048,128]{1,0:T(8,128)(2,1)S(1)}, u32[]{:S(2)}, u32[]{:S(2)}) collective-permute-start(bf16[2048,128]{1,0:T(8,128)(2,1)} %collective-permute-done.7.refs_9_), channel_id=1, source_target_pairs={{0,8},{8,0},{1,9},{9,1},{2,10},{10,2},{3,11},{11,3},{4,12},{12,4},... | collective-permute-start | bytes 1572872 | tf_op jit(solution)/shard_map/ppermute | solution.py:257
  45.2 10.8 %copy-start.4 = (bf16[512,512]{1,0:T(8,128)(2,1)}, bf16[512,512]{1,0:T(8,128)(2,1)S(1)}, u32[]{:S(2)}) copy-start(bf16[512,512]{1,0:T(8,128)(2,1)S(1)} %collective-permute-done.3.refs_0_.refs_2_) | copy-start | bytes 1572868
  45.2 10.8 %copy-start.5 = (bf16[512,512]{1,0:T(8,128)(2,1)}, bf16[512,512]{1,0:T(8,128)(2,1)S(1)}, u32[]{:S(2)}) copy-start(bf16[512,512]{1,0:T(8,128)(2,1)S(1)} %collective-permute-done.4.refs_1_.refs_5_) | copy-start | bytes 1572868
  50.5 5.6 %copy-start.1 = (bf16[2048,128]{1,0:T(8,128)(2,1)}, bf16[2048,128]{1,0:T(8,128)(2,1)S(1)}, u32[]{:S(2)}) copy-start(bf16[2048,128]{1,0:T(8,128)(2,1)S(1)} %collective-permute-done.8.rest_1_.refs_10_) | copy-start | bytes 1572868
  56.1 3.6 %copy-start.8 = (bf16[4096]{0:T(1024)(128)(2,1)S(1)}, bf16[4096]{0:T(1024)(128)(2,1)}, u32[]{:S(2)}) copy-start(bf16[4096]{0:T(1024)(128)(2,1)} %param.12) | copy-start | bytes 24580
  56.1 31.4 %all-to-all-start.2 = ((bf16[8,256,512]{2,1,0:T(8,128)(2,1)}), bf16[8,256,512]{2,1,0:T(8,128)(2,1)S(1)}, u32[]{:S(2)}, u32[]{:S(2)}) async-start(bf16[8,256,512]{2,1,0:T(8,128)(2,1)} %repeat_rows.1), calls=%async_computation.2 | async-start | bytes 4194304 | tf_op jit(solution)/shard_map/all_to_all | solution.py:265
  59.7 10.2 %copy-start.9 = (s32[32]{0:T(128)S(1)}, s32[32]{0:T(128)}, u32[]{:S(2)}) copy-start(s32[32]{0:T(128)} %param.18) | copy-start | bytes 388
  66.3 28.3 %collective-permute-start.9 = (bf16[1024,256]{1,0:T(8,128)(2,1)}, bf16[1024,256]{1,0:T(8,128)(2,1)}, u32[]{:S(2)}, u32[]{:S(2)}) collective-permute-start(bf16[1024,256]{1,0:T(8,128)(2,1)} %get-tuple-element.21), channel_id=1, source_target_pairs={{0,4},{4,0},{1,5},{5,1},{2,6},{6,2},{3,7},{7,3},{8,12},{12,8},{9,1... | collective-permute-start | bytes 1572872 | tf_op jit(solution)/shard_map/ppermute | solution.py:257
  70.5 24.1 %collective-permute-start.10 = (f32[8,128]{1,0:T(8,128)}, f32[8,128]{1,0:T(8,128)}, u32[]{:S(2)}, u32[]{:S(2)}) collective-permute-start(f32[8,128]{1,0:T(8,128)} %get-tuple-element.22.squares), channel_id=1, source_target_pairs={{0,4},{4,0},{1,5},{5,1},{2,6},{6,2},{3,7},{7,3},{8,12},{12,8},{9,1... | collective-permute-start | bytes 12296 | tf_op jit(solution)/shard_map/ppermute | solution.py:257
  87.4 7.2 %copy-start = (bf16[512,4096]{1,0:T(8,128)(2,1)S(1)}, bf16[512,4096]{1,0:T(8,128)(2,1)}, u32[]{:S(2)}) copy-start(bf16[512,4096]{1,0:T(8,128)(2,1)} %w_out.1) | copy-start | bytes 12582916
  128.5 18.1 %copy-start.7 = (s32[16,2,1,1]{0,1,3,2:T(2,128)S(1)}, s32[16,2,1,1]{0,1,3,2:T(2,128)}, u32[]{:S(2)}) copy-start(s32[16,2,1,1]{0,1,3,2:T(2,128)} %copy-done.6) | copy-start | bytes 388
  146.6 1.5 collective-permute-start.11
  (1 other events, 3.1 us)

commit v4 on v3

--- a/solution.py
+++ b/solution.py
@@ -31,6 +31,10 @@
     return pltpu.with_memory_space_constraint(x, pltpu.HBM)
 
 
+def in_vmem(x):
+    return pltpu.with_memory_space_constraint(x, pltpu.VMEM)
+
+
 def params(mib):
     return pltpu.CompilerParams(vmem_limit_bytes=mib << 20)
 
@@ -60,13 +64,14 @@
 
 
 def prefix_kernel(where, gain, *refs):
-    blocks, weights, (own, back, squares, x, w, acc, x_sem, w_sem) = refs[:7], refs[7:11], refs[11:]
-    xh, y, c = where[0], where[1], where[2]
+    blocks, weights, (own, back, squares, x, w, acc, x_sem, w_sem) = refs[:7], refs[7:10], refs[10:]
+    xh, y = where[0], where[1]
     parts, rows, part = x.shape
     w_copies = []
     for k, b in enumerate(weights):
         source = b.at[pl.ds(pl.multiple_of(xh * parts * part, part), parts * part), :] if k < 2 else b
-        w_copies.append(pltpu.make_async_copy(source, w.at[:, pl.ds(k * HEAD_DIM, HEAD_DIM)], w_sem.at[k]))
+        place = w.at[:, pl.ds(k * HEAD_DIM, b.shape[1])]
+        w_copies.append(pltpu.make_async_copy(source, place, w_sem.at[k]))
     middle = rows // 2
     places = [x.at[0]] + [x.at[k, pl.ds(r * middle, middle), :] for k in (1, 2, 3) for r in (0, 1)]
     x_copies = [pltpu.make_async_copy(b, p, x_sem.at[k]) for k, (b, p) in enumerate(zip(blocks, places))]
@@ -90,10 +95,7 @@
         else:
             acc[...] += term
     own[...] = acc[:, : 2 * HEAD_DIM]
-    a = acc[:, 2 * HEAD_DIM : 3 * HEAD_DIM].astype(BF16)
-    b = acc[:, 3 * HEAD_DIM :].astype(BF16)
-    back[:, :HEAD_DIM] = jnp.where(c == 0, a, b)
-    back[:, HEAD_DIM:] = jnp.where(c == 0, b, a)
+    back[...] = acc[:, 2 * HEAD_DIM :].astype(BF16)
     eye = unit(HEAD_DIM)
     for r in range(rows // HEAD_DIM):
         squares[r : r + 1, :] = to_row(total[r * HEAD_DIM : (r + 1) * HEAD_DIM], eye)
@@ -179,12 +181,10 @@
         pltpu.make_async_copy(prefix.at[pl.ds(0, middle), :], top, sem.at[0]),
         pltpu.make_async_copy(prefix.at[pl.ds(middle, middle), :], bottom, sem.at[1]),
     ]
-    key = pltpu.make_async_copy(w_k.at[rows, :], w_half, sem.at[2])
-    value = pltpu.make_async_copy(w_v.at[rows, :], w_half, sem.at[2])
+    halves.append(pltpu.make_async_copy(w_k.at[rows, :], w_half.at[:, pl.ds(0, HEAD_DIM)], sem.at[2]))
+    halves.append(pltpu.make_async_copy(w_v.at[rows, :], w_half.at[:, pl.ds(HEAD_DIM, HEAD_DIM)], sem.at[3]))
     for copy in halves:
         copy.start()
-    pl.when(where[2] == 0)(key.start)
-    pl.when(where[2] != 0)(value.start)
     eye = unit(length)
     lane = lax.broadcasted_iota(jnp.int32, (length, HEAD_DIM), 1)
     for s in range(slots):
@@ -194,7 +194,6 @@
         out[:, s, :, part:] = meta.reshape(pieces, 8, HEAD_DIM).astype(BF16)
     for copy in halves:
         copy.wait()
-    key.wait()
 
 
 def select_kernel(index, own, other, *rest):
@@ -301,12 +300,12 @@
             jax.ShapeDtypeStruct((chips, slots, piece, part + HEAD_DIM), BF16),
             jax.ShapeDtypeStruct((middle, part), BF16),
             jax.ShapeDtypeStruct((middle, part), BF16),
-            jax.ShapeDtypeStruct((half, HEAD_DIM), BF16),
+            jax.ShapeDtypeStruct((half, 2 * HEAD_DIM), BF16),
         ],
         in_specs=[smem(), smem(), vmem(), vmem()] + [anywhere()] * 3,
         out_specs=[vmem()] * 4,
-        scratch_shapes=[pltpu.SemaphoreType.DMA((3,))],
-        compiler_params=params(10),
+        scratch_shapes=[pltpu.SemaphoreType.DMA((4,))],
+        compiler_params=params(12),
         cost_estimate=pl.CostEstimate(flops=0, bytes_accessed=4 << 20, transcendentals=0),
         name="pack_states",
     )(place, in_hbm(scored_prompt), *[in_hbm(x) for x in (state_hidden, state_mask, prefix, w_key, w_value)])
@@ -315,7 +314,6 @@
     second = [turn(bottom, 1), turn(top, 3), turn(first[0], 1), turn(first[1], 3)]
     blocks = [prefix, first[0], second[0], second[2], second[3], second[1], first[1]]
     w_a = swap(w_send, "xh")
-    w_b = swap(w_a, "c")
 
     here = spread(packed, CHIPS)
     there = swap(here, "c")
@@ -331,7 +329,7 @@
     outward = jnp.where(ids % 2 == c, ids // 2, chips + ids // 2)
     routed = spread(select(inward, here, there, [mark(first, 10**9)]), CHIPS).reshape(rows, part + HEAD_DIM)
 
-    wide = repeat(routed, parts, part, [mark(second, 10**9), w_b])
+    wide = repeat(routed, parts, part, [mark(second, 10**9), w_a])
     wide = spread(wide, TENSOR)
     own, back, squares = pl.pallas_call(
         prefix_kernel,
@@ -340,7 +338,7 @@
             jax.ShapeDtypeStruct((length_p, 2 * HEAD_DIM), BF16),
             jax.ShapeDtypeStruct((length_p // HEAD_DIM, HEAD_DIM), F32),
         ],
-        in_specs=[smem(), vmem()] + [anywhere()] * 11,
+        in_specs=[smem(), vmem()] + [anywhere()] * 10,
         out_specs=[vmem()] * 3,
         scratch_shapes=[
             pltpu.VMEM((4, length_p, part), BF16),
@@ -352,7 +350,7 @@
         compiler_params=params(18),
         cost_estimate=pl.CostEstimate(flops=2147483648, bytes_accessed=8 << 20, transcendentals=0),
         name="prefix_projection",
-    )(place, gain, *[in_hbm(x) for x in [*blocks, w_key, w_value, w_a, w_b]])
+    )(place, gain, *[in_hbm(x) for x in [*blocks, w_key, w_value, w_a]])
     far, far_squares = swap(back, "xh"), swap(squares, "xh")
 
     q, k, v = pl.pallas_call(
@@ -386,7 +384,7 @@
         compiler_params=params(24),
         cost_estimate=pl.CostEstimate(flops=1800000000, bytes_accessed=8 << 20, transcendentals=1310720),
         name="attention",
-    )(limit[None], q, own, far, squares, far_squares, k, v, routed[:, part:], w_out)
+    )(limit[None], q, own, in_vmem(far), in_vmem(squares), in_vmem(far_squares), k, v, routed[:, part:], w_out)
 
     mixed = jnp.sum(spread(terms, TENSOR).astype(F32), axis=0).astype(BF16)
     here = spread(mixed.reshape(chips, slots, piece, part), CHIPS)

time: 165 us -> 164 us (level)
  blocking collectives: 60.5 us -> 58 us
  waiting for transfers between devices: 39.1 us -> 40.8 us
    ppermute x6 -> x5, waiting for transfers between devices: 3.08 us -> 7.46 us  [swap(): return lax.ppermute(x, axis, [(0, 1), (1, 0)])]
    all_to_all x3, waiting for transfers between devices: 25.7 us -> 22.9 us  [spread(): return lax.all_to_all(x, axis, 0, 0, tiled=True)]
    all_to_all x3, blocking collectives: 60.5 us -> 58 us  [spread(): return lax.all_to_all(x, axis, 0, 0, tiled=True)]
    ppermute x6 -> x5, starting transfers between devices: 6.44 us -> 6.39 us  [swap(): return lax.ppermute(x, axis, [(0, 1), (1, 0)])]
  transfers between devices with their start and end apart: 15 -> 14, of which waited for: 7 -> 8; matrix products, arithmetic and copies ran while one was open for 1% -> 1% of each run, Pallas kernels for 8% -> 8%
where the time goes in v4:
time: 164 us; the launch traced here: 163 us
  blocking collectives  58 us (35%)
  waiting for transfers between devices  40.8 us (25%)
  starting transfers between devices  37.2 us (23%)
  Pallas kernels  24.9 us (15%)
  local copies, waits for them, and re-layouts  1.7 us (1%)
    all_to_all x3, blocking collectives, spread(): return lax.all_to_all(x, axis, 0, 0, tiled=True)  58 us
    all_to_all x3, waiting for transfers between devices, spread(): return lax.all_to_all(x, axis, 0, 0, tiled=True)  22.9 us
    all_to_all x3, starting transfers between devices, spread(): return lax.all_to_all(x, axis, 0, 0, tiled=True)  22.3 us
    ppermute x6, waiting for transfers between devices, turn(): return lax.ppermute(x, 'y', [(i, (i + s) % 4) for i in range(4)])  10.4 us
    ppermute x6, starting transfers between devices, turn(): return lax.ppermute(x, 'y', [(i, (i + s) % 4) for i in range(4)])  8.56 us
    ppermute x5, waiting for transfers between devices, swap(): return lax.ppermute(x, axis, [(0, 1), (1, 0)])  7.46 us
    pallas_call x1, Pallas kernels, per_device(): pl.pallas_call(prefix_kernel, out_shape=[jax.ShapeDtypeStruct((length_p,...  6.61 us
    ppermute x5, starting transfers between devices, swap(): return lax.ppermute(x, axis, [(0, 1), (1, 0)])  6.39 us
  transfers between devices with their start and end apart: 14, of which 8 were waited for; matrix products, arithmetic and copies ran while one was open for 1% of the time, Pallas kernels for 8%

profile of v4, /device:TPU:32, one launch (start us, length us, event | category | flops | bytes accessed | tf_op | source)
XLA Modules:
  0.0 163.4 jit_solution(10197854469811193156)
XLA Ops:
  0.1 3.6 %pack_states.1 = (bf16[16,2,8,640]{3,2,1,0:T(8,128)(2,1)}, bf16[512,512]{1,0:T(8,128)(2,1)}, bf16[512,512]{1,0:T(8,128)(2,1)}, bf16[2048,256]{1,0:T(8,128)(2,1)S(1)}) custom-call(s32[3]{0:T(128)S(1)} %pad_add_fusion.where, s32[1,2]{1,0:T(1,128)} %ids.1, bf16[2,128,512]{2,1,0:T(8,128)(2,1)} %hidden.1, s32[2,128]{1,0:T(2,128)} %mask.1, ...), custom_call_target="tpu_custom_call" | custom-call | bytes 4194304 | tf_op jit(solution)/shard_map/pack_states/pallas_call | solution.py:297
  3.7 9.5 %all-to-all-start = ((bf16[16,2,8,640]{3,2,1,0:T(8,128)(2,1)}), bf16[16,2,8,640]{3,2,1,0:T(8,128)(2,1)S(1)}, u32[]{:S(2)}, u32[]{:S(2)}) async-start(bf16[16,2,8,640]{3,2,1,0:T(8,128)(2,1)} %get-tuple-element.15), calls=%async_computation | async-start | bytes 655360 | tf_op jit(solution)/shard_map/all_to_all | solution.py:264
  13.2 1.6 collective-permute-start.1
  14.8 1.7 %collective-permute-start.2 = (bf16[512,512]{1,0:T(8,128)(2,1)}, bf16[512,512]{1,0:T(8,128)(2,1)}, u32[]{:S(2)}, u32[]{:S(2)}) collective-permute-start(bf16[512,512]{1,0:T(8,128)(2,1)} %get-tuple-element.17), channel_id=1, source_target_pairs={{0,3},{1,0},{2,1},{3,2},{4,7},{5,4},{6,5},{7,6},{8,11},{9,8},{10,9... | collective-permute-start | bytes 1572872 | tf_op jit(solution)/shard_map/ppermute | solution.py:260
  16.4 1.8 %collective-permute-start.4 = (bf16[512,512]{1,0:T(8,128)(2,1)}, bf16[512,512]{1,0:T(8,128)(2,1)}, u32[]{:S(2)}, u32[]{:S(2)}) collective-permute-start(bf16[512,512]{1,0:T(8,128)(2,1)} %get-tuple-element.16), channel_id=1, source_target_pairs={{0,3},{1,0},{2,1},{3,2},{4,7},{5,4},{6,5},{7,6},{8,11},{9,8},{10,9... | collective-permute-start | bytes 1572872 | tf_op jit(solution)/shard_map/ppermute | solution.py:260
  18.5 5.9 %all-to-all-done.own = bf16[16,2,8,640]{3,2,1,0:T(8,128)(2,1)S(1)} async-done(((bf16[16,2,8,640]{3,2,1,0:T(8,128)(2,1)}), bf16[16,2,8,640]{3,2,1,0:T(8,128)(2,1)S(1)}, u32[]{:S(2)}, u32[]{:S(2)}) %all-to-all-start) | async-done | bytes 327712 | tf_op jit(solution)/shard_map/all_to_all | solution.py:264
  24.4 5.2 %collective-permute-done.1.refs_0_.refs_1_ = bf16[512,512]{1,0:T(8,128)(2,1)} collective-permute-done((bf16[512,512]{1,0:T(8,128)(2,1)}, bf16[512,512]{1,0:T(8,128)(2,1)}, u32[]{:S(2)}, u32[]{:S(2)}) %collective-permute-start.1) | collective-permute-done | bytes 524320 | tf_op jit(solution)/shard_map/ppermute | solution.py:260
  29.6 2.7 %collective-permute-start.7 = (bf16[2048,256]{1,0:T(8,128)(2,1)S(1)}, bf16[2048,256]{1,0:T(8,128)(2,1)S(1)}, u32[]{:S(2)}, u32[]{:S(2)}) collective-permute-start(bf16[2048,256]{1,0:T(8,128)(2,1)S(1)} %get-tuple-element.18), channel_id=1, source_target_pairs={{0,4},{4,0},{1,5},{5,1},{2,6},{6,2},{3,7},{7,3},{8,12},{12,8},{9,1... | collective-permute-start | bytes 3145736 | tf_op jit(solution)/shard_map/ppermute | solution.py:256
  32.8 2.9 %collective-permute-start.6 = (bf16[512,512]{1,0:T(8,128)(2,1)}, bf16[512,512]{1,0:T(8,128)(2,1)}, u32[]{:S(2)}, u32[]{:S(2)}) collective-permute-start(bf16[512,512]{1,0:T(8,128)(2,1)} %collective-permute-done.2.refs_1_.refs_6_), channel_id=1, source_target_pairs={{0,3},{1,0},{2,1},{3,2},{4,7},{5,4},{6,5},{7,6},{8,11},{9,8},{10,9... | collective-permute-start | bytes 1572872 | tf_op jit(solution)/shard_map/ppermute | solution.py:260
  36.1 1.5 select_blocks.2
  37.6 7.5 %all-to-all-start.1 = ((bf16[16,2,8,640]{3,2,1,0:T(8,128)(2,1)}), bf16[16,2,8,640]{3,2,1,0:T(8,128)(2,1)S(1)}, u32[]{:S(2)}, u32[]{:S(2)}) async-start(bf16[16,2,8,640]{3,2,1,0:T(8,128)(2,1)} %select_blocks.2), calls=%async_computation.1 | async-start | bytes 655360 | tf_op jit(solution)/shard_map/all_to_all | solution.py:264
  45.1 5.2 %collective-permute-done.5.refs_2_.refs_3_ = bf16[512,512]{1,0:T(8,128)(2,1)} collective-permute-done((bf16[512,512]{1,0:T(8,128)(2,1)}, bf16[512,512]{1,0:T(8,128)(2,1)}, u32[]{:S(2)}, u32[]{:S(2)}) %collective-permute-start.5) | collective-permute-done | bytes 524320 | tf_op jit(solution)/shard_map/ppermute | solution.py:260
  50.4 5.8 %collective-permute-done.7.rest_1_.refs_9_ = bf16[2048,256]{1,0:T(8,128)(2,1)S(1)} collective-permute-done((bf16[2048,256]{1,0:T(8,128)(2,1)S(1)}, bf16[2048,256]{1,0:T(8,128)(2,1)S(1)}, u32[]{:S(2)}, u32[]{:S(2)}) %collective-permute-start.7) | collective-permute-done | bytes 1048608 | tf_op jit(solution)/shard_map/ppermute | solution.py:256
  56.4 1.5 repeat_rows.1
  57.9 5.2 %all-to-all-start.2 = ((bf16[8,256,512]{2,1,0:T(8,128)(2,1)}), bf16[8,256,512]{2,1,0:T(8,128)(2,1)S(1)}, u32[]{:S(2)}, u32[]{:S(2)}) async-start(bf16[8,256,512]{2,1,0:T(8,128)(2,1)} %repeat_rows.1), calls=%async_computation.2 | async-start | bytes 4194304 | tf_op jit(solution)/shard_map/all_to_all | solution.py:264
  63.2 6.6 %prefix_projection.1 = (f32[1024,256]{1,0:T(8,128)S(1)}, bf16[1024,256]{1,0:T(8,128)(2,1)}, f32[8,128]{1,0:T(8,128)}) custom-call(s32[3]{0:T(128)S(1)} %pad_add_fusion.where, bf16[8,1,512]{2,1,0:T(2,128)(2,1)S(1)} %reshape.42.gain, bf16[1024,512]{1,0:T(8,128)(2,1)} %bitcast.16, bf16[512,512]{1,0:T(8,128)(2,1)} %collective-permute-done.1.refs_0_.refs_1_, ...), custom_call_target="tpu_custom_call" | custom-call | flops 2147483648 | bytes 8388608 | tf_op jit(solution)/shard_map/prefix_projection/pallas_call | solution.py:334
  69.8 3.6 %collective-permute-start.8 = (bf16[1024,256]{1,0:T(8,128)(2,1)}, bf16[1024,256]{1,0:T(8,128)(2,1)}, u32[]{:S(2)}, u32[]{:S(2)}) collective-permute-start(bf16[1024,256]{1,0:T(8,128)(2,1)} %get-tuple-element.21), channel_id=1, source_target_pairs={{0,4},{4,0},{1,5},{5,1},{2,6},{6,2},{3,7},{7,3},{8,12},{12,8},{9,1... | collective-permute-start | bytes 1572872 | tf_op jit(solution)/shard_map/ppermute | solution.py:256
  74.0 16.7 %all-to-all-done.2.x = bf16[8,256,512]{2,1,0:T(8,128)(2,1)S(1)} async-done(((bf16[8,256,512]{2,1,0:T(8,128)(2,1)}), bf16[8,256,512]{2,1,0:T(8,128)(2,1)S(1)}, u32[]{:S(2)}, u32[]{:S(2)}) %all-to-all-start.2) | async-done | bytes 2097184 | tf_op jit(solution)/shard_map/all_to_all | solution.py:264
  90.7 5.5 %state_projection.1 = (bf16[256,512]{1,0:T(8,128)(2,1)S(1)}, bf16[256,128]{1,0:T(8,128)(2,1)S(1)}, bf16[256,128]{1,0:T(8,128)(2,1)S(1)}) custom-call(bf16[8,256,512]{2,1,0:T(8,128)(2,1)S(1)} %all-to-all-done.2.x, bf16[8,1,512]{2,1,0:T(2,128)(2,1)S(1)} %reshape.42.gain, bf16[4096,512]{1,0:T(8,128)(2,1)} %w_q.1, bf16[4096,128]{1,0:T(8,128)(2,1)} %refs_7_.1, ...), custom_call_target="tpu_custom_call" | custom-call | flops 1610612736 | bytes 8388608 | tf_op jit(solution)/shard_map/state_projection/pallas_call | solution.py:356
  96.5 5.5 %attention.1 = bf16[8,256,512]{2,1,0:T(8,128)(2,1)S(1)} custom-call(s32[1]{0:T(128)} %dynamic_slice.4.limit, bf16[256,512]{1,0:T(8,128)(2,1)S(1)} %get-tuple-element.19.q, f32[1024,256]{1,0:T(8,128)S(1)} %get-tuple-element.20.own, bf16[1024,256]{1,0:T(8,128)(2,1)} %collective-permute-done.8.far, f32[8,128]{1,0:T(8,128)} %get-tuple-element.22.squares, ...), custom_call_target="tpu_custom_call" | custom-call | flops 1800000000 | bytes 8388608 | tf_op jit(solution)/shard_map/attention/pallas_call | solution.py:375
  102.1 27.1 %all_to_all.30 = bf16[8,256,512]{2,1,0:T(8,128)(2,1)S(1)} all-to-all(bf16[8,256,512]{2,1,0:T(8,128)(2,1)S(1)} %attention.1), channel_id=1, replica_groups=mesh['xl'=2,'z'=8,'c'=2,'xh'=2,'y'=4] {'xh','y'}, dimensions={0} | all-to-all | bytes 4194304 | tf_op jit(solution)/shard_map/all_to_all | solution.py:264
  129.5 16.6 %all_to_all.31.own = bf16[16,2,8,512]{3,2,1,0:T(8,128)(2,1)S(1)} all-to-all(bf16[16,2,8,512]{3,2,1,0:T(8,128)(2,1)S(1)} %bitcast.17), channel_id=1, replica_groups=mesh['xl'=2,'z'=8,'c'=2,'xh'=2,'y'=4] {'xl','z'}, dimensions={0} | all-to-all | bytes 524288 | tf_op jit(solution)/shard_map/all_to_all | solution.py:264
  146.2 1.4 collective-permute-done.10.other
  148.4 14.4 %all_to_all.32 = bf16[16,2,8,512]{3,2,1,0:T(8,128)(2,1)S(1)} all-to-all(bf16[16,2,8,512]{3,2,1,0:T(8,128)(2,1)S(1)} %select_blocks.3), channel_id=1, replica_groups=mesh['xl'=2,'z'=8,'c'=2,'xh'=2,'y'=4] {'xl','z'}, dimensions={0} | all-to-all | bytes 524288 | tf_op jit(solution)/shard_map/all_to_all | solution.py:264
  (43 shorter events, 4.3 us)
Async XLA Ops:
  3.7 20.7 %all-to-all-start = ((bf16[16,2,8,640]{3,2,1,0:T(8,128)(2,1)}), bf16[16,2,8,640]{3,2,1,0:T(8,128)(2,1)S(1)}, u32[]{:S(2)}, u32[]{:S(2)}) async-start(bf16[16,2,8,640]{3,2,1,0:T(8,128)(2,1)} %get-tuple-element.15), calls=%async_computation | async-start | bytes 655360 | tf_op jit(solution)/shard_map/all_to_all | solution.py:264
  13.2 16.4 %collective-permute-start.1 = (bf16[512,512]{1,0:T(8,128)(2,1)}, bf16[512,512]{1,0:T(8,128)(2,1)}, u32[]{:S(2)}, u32[]{:S(2)}) collective-permute-start(bf16[512,512]{1,0:T(8,128)(2,1)} %get-tuple-element.16), channel_id=1, source_target_pairs={{0,1},{1,2},{2,3},{3,0},{4,5},{5,6},{6,7},{7,4},{8,9},{9,10},{10,1... | collective-permute-start | bytes 1572872 | tf_op jit(solution)/shard_map/ppermute | solution.py:260
  14.8 17.5 %collective-permute-start.2 = (bf16[512,512]{1,0:T(8,128)(2,1)}, bf16[512,512]{1,0:T(8,128)(2,1)}, u32[]{:S(2)}, u32[]{:S(2)}) collective-permute-start(bf16[512,512]{1,0:T(8,128)(2,1)} %get-tuple-element.17), channel_id=1, source_target_pairs={{0,3},{1,0},{2,1},{3,2},{4,7},{5,4},{6,5},{7,6},{8,11},{9,8},{10,9... | collective-permute-start | bytes 1572872 | tf_op jit(solution)/shard_map/ppermute | solution.py:260
  16.4 28.7 %collective-permute-start.4 = (bf16[512,512]{1,0:T(8,128)(2,1)}, bf16[512,512]{1,0:T(8,128)(2,1)}, u32[]{:S(2)}, u32[]{:S(2)}) collective-permute-start(bf16[512,512]{1,0:T(8,128)(2,1)} %get-tuple-element.16), channel_id=1, source_target_pairs={{0,3},{1,0},{2,1},{3,2},{4,7},{5,4},{6,5},{7,6},{8,11},{9,8},{10,9... | collective-permute-start | bytes 1572872 | tf_op jit(solution)/shard_map/ppermute | solution.py:260
  18.2 26.9 %collective-permute-start.3 = (bf16[512,512]{1,0:T(8,128)(2,1)}, bf16[512,512]{1,0:T(8,128)(2,1)}, u32[]{:S(2)}, u32[]{:S(2)}) collective-permute-start(bf16[512,512]{1,0:T(8,128)(2,1)} %get-tuple-element.17), channel_id=1, source_target_pairs={{0,1},{1,2},{2,3},{3,0},{4,5},{5,6},{6,7},{7,4},{8,9},{9,10},{10,1... | collective-permute-start | bytes 1572872 | tf_op jit(solution)/shard_map/ppermute | solution.py:260
  24.4 8.4 %collective-permute-start = (bf16[16,2,8,640]{3,2,1,0:T(8,128)(2,1)S(1)}, bf16[16,2,8,640]{3,2,1,0:T(8,128)(2,1)S(1)}, u32[]{:S(2)}, u32[]{:S(2)}) collective-permute-start(bf16[16,2,8,640]{3,2,1,0:T(8,128)(2,1)S(1)} %all-to-all-done.own), channel_id=1, source_target_pairs={{0,8},{8,0},{1,9},{9,1},{2,10},{10,2},{3,11},{11,3},{4,12},{12,4},... | collective-permute-start | bytes 983048 | tf_op jit(solution)/shard_map/ppermute | solution.py:256
  29.6 26.6 %collective-permute-start.7 = (bf16[2048,256]{1,0:T(8,128)(2,1)S(1)}, bf16[2048,256]{1,0:T(8,128)(2,1)S(1)}, u32[]{:S(2)}, u32[]{:S(2)}) collective-permute-start(bf16[2048,256]{1,0:T(8,128)(2,1)S(1)} %get-tuple-element.18), channel_id=1, source_target_pairs={{0,4},{4,0},{1,5},{5,1},{2,6},{6,2},{3,7},{7,3},{8,12},{12,8},{9,1... | collective-permute-start | bytes 3145736 | tf_op jit(solution)/shard_map/ppermute | solution.py:256
  32.3 18.0 %collective-permute-start.5 = (bf16[512,512]{1,0:T(8,128)(2,1)}, bf16[512,512]{1,0:T(8,128)(2,1)}, u32[]{:S(2)}, u32[]{:S(2)}) collective-permute-start(bf16[512,512]{1,0:T(8,128)(2,1)} %collective-permute-done.1.refs_0_.refs_1_), channel_id=1, source_target_pairs={{0,1},{1,2},{2,3},{3,0},{4,5},{5,6},{6,7},{7,4},{8,9},{9,10},{10,1... | collective-permute-start | bytes 1572872 | tf_op jit(solution)/shard_map/ppermute | solution.py:260
  32.8 3.0 %copy-start.2 = (s32[16,2,1,1]{0,1,3,2:T(2,128)}, s32[16,2,1,1]{0,1,3,2:T(2,128)S(1)}, u32[]{:S(2)}) copy-start(s32[16,2,1,1]{0,1,3,2:T(2,128)S(1)} %copy.40) | copy-start | bytes 388
  32.8 17.6 %collective-permute-start.6 = (bf16[512,512]{1,0:T(8,128)(2,1)}, bf16[512,512]{1,0:T(8,128)(2,1)}, u32[]{:S(2)}, u32[]{:S(2)}) collective-permute-start(bf16[512,512]{1,0:T(8,128)(2,1)} %collective-permute-done.2.refs_1_.refs_6_), channel_id=1, source_target_pairs={{0,3},{1,0},{2,1},{3,2},{4,7},{5,4},{6,5},{7,6},{8,11},{9,8},{10,9... | collective-permute-start | bytes 1572872 | tf_op jit(solution)/shard_map/ppermute | solution.py:260
  37.6 18.8 %all-to-all-start.1 = ((bf16[16,2,8,640]{3,2,1,0:T(8,128)(2,1)}), bf16[16,2,8,640]{3,2,1,0:T(8,128)(2,1)S(1)}, u32[]{:S(2)}, u32[]{:S(2)}) async-start(bf16[16,2,8,640]{3,2,1,0:T(8,128)(2,1)} %select_blocks.2), calls=%async_computation.1 | async-start | bytes 655360 | tf_op jit(solution)/shard_map/all_to_all | solution.py:264
  56.2 1.8 %copy-start.1 = (bf16[2048,256]{1,0:T(8,128)(2,1)}, bf16[2048,256]{1,0:T(8,128)(2,1)S(1)}, u32[]{:S(2)}) copy-start(bf16[2048,256]{1,0:T(8,128)(2,1)S(1)} %collective-permute-done.7.rest_1_.refs_9_) | copy-start | bytes 3145732
  57.9 5.2 %copy-start.4 = (bf16[4096]{0:T(1024)(128)(2,1)S(1)}, bf16[4096]{0:T(1024)(128)(2,1)}, u32[]{:S(2)}) copy-start(bf16[4096]{0:T(1024)(128)(2,1)} %param.12) | copy-start | bytes 24580
  57.9 32.8 %all-to-all-start.2 = ((bf16[8,256,512]{2,1,0:T(8,128)(2,1)}), bf16[8,256,512]{2,1,0:T(8,128)(2,1)S(1)}, u32[]{:S(2)}, u32[]{:S(2)}) async-start(bf16[8,256,512]{2,1,0:T(8,128)(2,1)} %repeat_rows.1), calls=%async_computation.2 | async-start | bytes 4194304 | tf_op jit(solution)/shard_map/all_to_all | solution.py:264
  63.1 10.2 %copy-start.5 = (s32[32]{0:T(128)S(1)}, s32[32]{0:T(128)}, u32[]{:S(2)}) copy-start(s32[32]{0:T(128)} %param.18) | copy-start | bytes 388
  69.8 26.7 %collective-permute-start.8 = (bf16[1024,256]{1,0:T(8,128)(2,1)}, bf16[1024,256]{1,0:T(8,128)(2,1)}, u32[]{:S(2)}, u32[]{:S(2)}) collective-permute-start(bf16[1024,256]{1,0:T(8,128)(2,1)} %get-tuple-element.21), channel_id=1, source_target_pairs={{0,4},{4,0},{1,5},{5,1},{2,6},{6,2},{3,7},{7,3},{8,12},{12,8},{9,1... | collective-permute-start | bytes 1572872 | tf_op jit(solution)/shard_map/ppermute | solution.py:256
  74.0 22.5 %collective-permute-start.9 = (f32[8,128]{1,0:T(8,128)}, f32[8,128]{1,0:T(8,128)}, u32[]{:S(2)}, u32[]{:S(2)}) collective-permute-start(f32[8,128]{1,0:T(8,128)} %get-tuple-element.22.squares), channel_id=1, source_target_pairs={{0,4},{4,0},{1,5},{5,1},{2,6},{6,2},{3,7},{7,3},{8,12},{12,8},{9,1... | collective-permute-start | bytes 12296 | tf_op jit(solution)/shard_map/ppermute | solution.py:256
  90.7 5.8 %copy-start = (bf16[512,4096]{1,0:T(8,128)(2,1)S(1)}, bf16[512,4096]{1,0:T(8,128)(2,1)}, u32[]{:S(2)}) copy-start(bf16[512,4096]{1,0:T(8,128)(2,1)} %w_out.1) | copy-start | bytes 12582916
  129.1 17.0 %copy-start.3 = (s32[16,2,1,1]{0,1,3,2:T(2,128)S(1)}, s32[16,2,1,1]{0,1,3,2:T(2,128)}, u32[]{:S(2)}) copy-start(s32[16,2,1,1]{0,1,3,2:T(2,128)} %copy-done.2) | copy-start | bytes 388
  146.1 1.5 collective-permute-start.10
